TPU v7x, 128 devices: a whole 4x4x4 slice. The times are simulated.
128 devices in a mesh: dp: 8 (over x_hi, y), tensor: 16 (over z, x_lo, core).
Axes of the slice: x: 4 (x_hi: 2, x_lo: 2; x = x_hi * 2 + x_lo), y: 4, z: 4, core: 2. Of those that a mesh axis runs over, the one named last changes fastest.
Arguments:
- inputs: bfloat16 [1024, 6144], P('dp'), may hold values from -6 to 6
- targets: bfloat16 [1024, 6144], P('dp'), may hold values from -6 to 6
- lengths: int32 [8], P('dp'), may hold values from 1 to 128, 768 in all
- ln_gain: float32 [6144], replicated, may hold values from 0.5 to 1.5
- ln_bias: float32 [6144], replicated, may hold values from -0.8 to 0.8
- query_weight: bfloat16 [6144, 6144], P(None, 'tensor'), may hold values from -0.078125 to 0.078125
- w_key: bfloat16 [6144, 6144], P(None, 'tensor'), may hold values from -0.078125 to 0.078125
- value_weight: bfloat16 [6144, 6144], P(None, 'tensor'), may hold values from -0.078125 to 0.078125
- w_out: bfloat16 [6144, 6144], P('tensor'), may hold values from -0.078125 to 0.078125
- down_query: bfloat16 [6144, 16], replicated, may hold values from -0.078125 to 0.078125
- down_value: bfloat16 [6144, 16], replicated, may hold values from -0.078125 to 0.078125
- query_up_factor: float32 [16, 6144], P(None, 'tensor'), may hold values from -0.6 to 0.6
- value_up_factor: float32 [16, 6144], P(None, 'tensor'), may hold values from -0.6 to 0.6
Outputs:
- step_query: float32 [16, 6144], P(None, 'tensor')
- step_value: float32 [16, 6144], P(None, 'tensor')
- remain_query: float32 [16, 6144], P(None, 'tensor')
- remain_value: float32 [16, 6144], P(None, 'tensor')
Inputs may be any that keep to these rules, and one draw needn't show every extreme that they name: `lengths`: live tokens of each sequence; one sequence has exactly 128.
All inputs are finite; a program needn't handle non-finite values. No bound on the sum of `lengths` on one device may be relied on, other than what follows from the above.
Results may differ from a plain program's by a relative error of at most 0.035.
Values sent between devices are 32-bit elements; how exact they have to be, the bound alone decides.
A program may use at most 128 MiB of HBM per device.

v0:
```python
import jax
import jax.numpy as jnp
from jax import lax
from jax.sharding import PartitionSpec as P

HEAD_DIM = 128
CG_STEPS = 3


EPS = 1e-05
ADAPTER_SCALE = 2.0
DAMP = 0.05
NEG = -1e30


def layer_norm(rows, gain, bias):
    rows = rows.astype(jnp.float32)
    centred = rows - jnp.mean(rows, axis=-1, keepdims=True)
    spread = jnp.mean(centred * centred, axis=-1, keepdims=True)
    return (centred * lax.rsqrt(spread + EPS) * gain + bias).astype(jnp.bfloat16)


def attend(
    ups, normalized_input, query_weight, w_key, value_weight, w_out, down_query, down_value, live
):
    query_up_factor, value_up_factor = ups
    length = normalized_input.shape[0]
    heads = query_weight.shape[1] // HEAD_DIM
    query_down_factor = jnp.dot(normalized_input, down_query, preferred_element_type=jnp.float32)
    value_down_factor = jnp.dot(normalized_input, down_value, preferred_element_type=jnp.float32)
    query_rows = jnp.dot(
        normalized_input, query_weight, preferred_element_type=jnp.float32
    ) + ADAPTER_SCALE * jnp.dot(query_down_factor, query_up_factor, precision=lax.Precision.HIGHEST)
    value_rows = jnp.dot(
        normalized_input, value_weight, preferred_element_type=jnp.float32
    ) + ADAPTER_SCALE * jnp.dot(value_down_factor, value_up_factor, precision=lax.Precision.HIGHEST)
    keys = jnp.dot(normalized_input, w_key, preferred_element_type=jnp.float32)
    query_rows = query_rows.astype(jnp.bfloat16).reshape(length, heads, HEAD_DIM)
    value_rows = value_rows.astype(jnp.bfloat16).reshape(length, heads, HEAD_DIM)
    keys = keys.astype(jnp.bfloat16).reshape(length, heads, HEAD_DIM)
    scores = jnp.einsum(
        "qhd,khd->hqk", query_rows, keys, preferred_element_type=jnp.float32
    ) * HEAD_DIM ** (-0.5)
    scores = jnp.where(live[None], scores, NEG)
    top = lax.stop_gradient(jnp.max(scores, axis=-1, keepdims=True))
    weights = jnp.exp(scores - top)
    probs = (weights / jnp.sum(weights, axis=-1, keepdims=True)).astype(jnp.bfloat16)
    mixed = jnp.einsum("hqk,khd->qhd", probs, value_rows, preferred_element_type=jnp.float32)
    mixed = mixed.astype(jnp.bfloat16).reshape(length, heads * HEAD_DIM)
    return jnp.dot(mixed, w_out, preferred_element_type=jnp.float32)


def linear_parts(apply, ups):
    output, pullback = jax.vjp(apply, ups)

    def backward(cotan):
        return pullback(cotan)[0]

    def forward(vector):
        _, undo = jax.vjp(backward, jnp.zeros_like(output))
        return undo(vector)[0]

    return (output, forward, backward)


def local_dot(first, second):
    return jnp.sum(first[0] * second[0]) + jnp.sum(first[1] * second[1])


def head_total(partial_value, offset, row_live):
    position = lax.axis_index("tensor")
    share = lax.psum_scatter(partial_value, "tensor", scatter_dimension=0, tiled=True)
    rows = share.shape[0]
    live_share = lax.dynamic_slice_in_dim(row_live, position * rows, rows, 0)
    if offset is not None:
        share = share + lax.dynamic_slice_in_dim(offset, position * rows, rows, 0)
    sent = live_share[:, None] * share
    return lax.all_gather(sent, "tensor", axis=0, tiled=True)


def on_device(
    inputs,
    targets,
    lengths,
    ln_gain,
    ln_bias,
    query_weight,
    w_key,
    value_weight,
    w_out,
    down_query,
    down_value,
    query_up_factor,
    value_up_factor,
):
    length = inputs.shape[0]
    places = jnp.arange(length, dtype=jnp.int32)
    limit = lengths[0]
    live = (places[None, :] <= places[:, None]) & (places[None, :] < limit)
    row_live = (places < limit).astype(jnp.float32)
    normalized_input = layer_norm(inputs, ln_gain, ln_bias)
    ups = (query_up_factor, value_up_factor)

    def apply(weights):
        return attend(
            weights,
            normalized_input,
            query_weight,
            w_key,
            value_weight,
            w_out,
            down_query,
            down_value,
            live,
        )

    output, linear, backward = linear_parts(apply, ups)
    token_count = length * lax.axis_size("dp")
    gap = inputs.astype(jnp.float32) - targets.astype(jnp.float32)

    def pulled(shared):
        return backward(shared / token_count)

    def data_sum(part):
        return lax.psum((part[0], part[1]), "dp")

    def squared(vector):
        return lax.psum(local_dot(vector, vector), "tensor")

    grads = data_sum(pulled(head_total(output, gap, row_live)))
    newton = (jnp.zeros_like(query_up_factor), jnp.zeros_like(value_up_factor))
    remain = (-grads[0], -grads[1])
    direction = remain
    norm_now = squared(remain)
    for index in range(CG_STEPS):
        part = pulled(head_total(linear(direction), None, row_live))
        summed = data_sum(part)
        image = (summed[0] + DAMP * direction[0], summed[1] + DAMP * direction[1])
        curv = lax.psum(local_dot(direction, image), "tensor")
        alpha = norm_now / curv
        newton = (newton[0] + alpha * direction[0], newton[1] + alpha * direction[1])
        remain = (remain[0] - alpha * image[0], remain[1] - alpha * image[1])
        norm_next = squared(remain)
        ratio = norm_next / norm_now
        direction = (remain[0] + ratio * direction[0], remain[1] + ratio * direction[1])
        norm_now = norm_next
    return (newton[0], newton[1], remain[0], remain[1])


def solution(mesh):
    in_specs = (
        P("dp", None),
        P("dp", None),
        P("dp"),
        P(),
        P(),
        P(None, "tensor"),
        P(None, "tensor"),
        P(None, "tensor"),
        P("tensor", None),
        P(),
        P(),
        P(None, "tensor"),
        P(None, "tensor"),
    )
    out_specs = (P(None, "tensor"), P(None, "tensor"), P(None, "tensor"), P(None, "tensor"))
    return jax.shard_map(
        on_device, mesh=mesh, in_specs=in_specs, out_specs=out_specs, check_vma=False
    )
```

profile of v0, /device:TPU:1, one launch (start us, length us, event | category | flops | bytes accessed | tf_op | source)
XLA Modules:
  0.0 824.5 jit_solution(12294876788159278559)
XLA Ops:
  28.2 5.1 fusion.153
  35.4 65.5 %reduce-scatter.5.cloned.1.call-done = f32[8,6144]{1,0:T(8,128)} async-done(((f32[128,6144]{1,0:T(8,128)}), f32[8,6144]{1,0:T(8,128)}) %reduce-scatter.5.cloned.1.call-update) | async-done | bytes 196624 | tf_op jit(solution)/shard_map/reduce_scatter | solution.py:72
  102.9 38.0 %all-gather.5.cloned.1.call-done = f32[128,6144]{1,0:T(8,128)} async-done(((f32[8,6144]{1,0:T(8,128)}), f32[128,6144]{1,0:T(8,128)}) %all-gather.5.cloned.1.call-update) | async-done | bytes 3145744 | tf_op jit(solution)/shard_map/all_gather | solution.py:78
  148.3 34.6 %all-reduce.4 = (f32[16,384]{1,0:T(8,128)S(1)}, f32[16,384]{1,0:T(8,128)S(1)}) all-reduce(f32[16,384]{1,0:T(8,128)S(1)} %fusion.154, f32[16,384]{1,0:T(8,128)S(1)} %fusion.155), channel_id=1, replica_groups=mesh['dp'=8,'tensor'=16] {'dp'}, use_global_device_ids=true, to_apply=%region_6.7 | all-reduce | flops 12288 | bytes 98304 | tf_op jit(solution)/shard_map/psum | solution.py:125
  185.6 5.0 fusion.157
  190.9 67.6 %reduce-scatter.7.cloned.1.call-done = f32[8,6144]{1,0:T(8,128)} async-done(((f32[128,6144]{1,0:T(8,128)}), f32[8,6144]{1,0:T(8,128)}) %reduce-scatter.7.cloned.1.call-update) | async-done | bytes 196624 | tf_op jit(solution)/shard_map/reduce_scatter | solution.py:72
  260.2 37.9 %all-gather.7.cloned.1.call-done = f32[128,6144]{1,0:T(8,128)} async-done(((f32[8,6144]{1,0:T(8,128)}), f32[128,6144]{1,0:T(8,128)}) %all-gather.7.cloned.1.call-update) | async-done | bytes 3145744 | tf_op jit(solution)/shard_map/all_gather | solution.py:78
  298.2 4.8 fusion.32
  305.6 34.6 %all-reduce.3 = (f32[16,384]{1,0:T(8,128)S(1)}, f32[16,384]{1,0:T(8,128)S(1)}) all-reduce(f32[16,384]{1,0:T(8,128)S(1)} %fusion.158, f32[16,384]{1,0:T(8,128)S(1)} %fusion.159), channel_id=1, replica_groups=mesh['dp'=8,'tensor'=16] {'dp'}, use_global_device_ids=true, to_apply=%region_14.15 | all-reduce | flops 12288 | bytes 98304 | tf_op jit(solution)/shard_map/psum | solution.py:125
  344.0 34.6 %all-reduce = (f32[]{:T(128)}, f32[]{:T(128)}) all-reduce(f32[]{:T(128)S(6)} %add.139, f32[]{:T(128)S(6)} %add.142), channel_id=1, replica_groups=mesh['dp'=8,'tensor'=16] {'tensor'}, use_global_device_ids=true, to_apply=%region_10.11 | all-reduce | flops 2 | bytes 16 | tf_op jit(solution)/shard_map/psum | solution.py:128
  382.5 27.6 %psum.104 = f32[]{:T(128)} all-reduce(f32[]{:T(128)S(6)} %add.143), channel_id=1, replica_groups=mesh['dp'=8,'tensor'=16] {'tensor'}, use_global_device_ids=true, to_apply=%region_21.22 | all-reduce | flops 1 | bytes 8 | tf_op jit(solution)/shard_map/psum | solution.py:128
  414.2 5.0 fusion.161
  419.3 59.3 %reduce-scatter.9.cloned.1.call-done = f32[8,6144]{1,0:T(8,128)} async-done(((f32[128,6144]{1,0:T(8,128)}), f32[8,6144]{1,0:T(8,128)}) %reduce-scatter.9.cloned.1.call-update) | async-done | bytes 196624 | tf_op jit(solution)/shard_map/reduce_scatter | solution.py:72
  480.4 37.5 %all-gather.9.cloned.1.call-done = f32[128,6144]{1,0:T(8,128)} async-done(((f32[8,6144]{1,0:T(8,128)}), f32[128,6144]{1,0:T(8,128)}) %all-gather.9.cloned.1.call-update) | async-done | bytes 3145744 | tf_op jit(solution)/shard_map/all_gather | solution.py:78
  518.0 4.8 fusion.35
  525.3 34.6 %all-reduce.2 = (f32[16,384]{1,0:T(8,128)S(1)}, f32[16,384]{1,0:T(8,128)S(1)}) all-reduce(f32[16,384]{1,0:T(8,128)S(1)} %fusion.162, f32[16,384]{1,0:T(8,128)S(1)} %fusion.163), channel_id=1, replica_groups=mesh['dp'=8,'tensor'=16] {'dp'}, use_global_device_ids=true, to_apply=%region_25.26 | all-reduce | flops 12288 | bytes 98304 | tf_op jit(solution)/shard_map/psum | solution.py:125
  562.5 34.6 %psum.107 = f32[]{:T(128)} all-reduce(f32[]{:T(128)S(6)} %add.148), channel_id=1, replica_groups=mesh['dp'=8,'tensor'=16] {'tensor'}, use_global_device_ids=true, to_apply=%region_29.30 | all-reduce | flops 1 | bytes 8 | tf_op jit(solution)/shard_map/psum | solution.py:139
  600.9 27.6 %psum.108 = f32[]{:T(128)} all-reduce(f32[]{:T(128)S(6)} %add.150), channel_id=1, replica_groups=mesh['dp'=8,'tensor'=16] {'tensor'}, use_global_device_ids=true, to_apply=%region_32.33 | all-reduce | flops 1 | bytes 8 | tf_op jit(solution)/shard_map/psum | solution.py:128
  632.6 5.0 fusion.165
  637.7 59.5 %reduce-scatter.11.cloned.1.call-done = f32[8,6144]{1,0:T(8,128)} async-done(((f32[128,6144]{1,0:T(8,128)}), f32[8,6144]{1,0:T(8,128)}) %reduce-scatter.11.cloned.1.call-update) | async-done | bytes 196624 | tf_op jit(solution)/shard_map/reduce_scatter | solution.py:72
  699.0 37.6 %all-gather.11.cloned.1.call-done = f32[128,6144]{1,0:T(8,128)} async-done(((f32[8,6144]{1,0:T(8,128)}), f32[128,6144]{1,0:T(8,128)}) %all-gather.11.cloned.1.call-update) | async-done | bytes 3145744 | tf_op jit(solution)/shard_map/all_gather | solution.py:78
  736.6 4.8 fusion.38
  743.9 34.6 %all-reduce.1 = (f32[16,384]{1,0:T(8,128)S(1)}, f32[16,384]{1,0:T(8,128)S(1)}) all-reduce(f32[16,384]{1,0:T(8,128)S(1)} %fusion.166, f32[16,384]{1,0:T(8,128)S(1)} %fusion.167), channel_id=1, replica_groups=mesh['dp'=8,'tensor'=16] {'dp'}, use_global_device_ids=true, to_apply=%region_36.37 | all-reduce | flops 12288 | bytes 98304 | tf_op jit(solution)/shard_map/psum | solution.py:125
  781.1 34.6 %psum.111 = f32[]{:T(128)} all-reduce(f32[]{:T(128)S(6)} %add.155), channel_id=1, replica_groups=mesh['dp'=8,'tensor'=16] {'tensor'}, use_global_device_ids=true, to_apply=%region_40.41 | all-reduce | flops 1 | bytes 8 | tf_op jit(solution)/shard_map/psum | solution.py:139
  (141 shorter events, 59.6 us)
Async XLA Ops:
  7.2 4.8 copy-start
  7.2 4.1 copy-start.1
  7.2 4.0 copy-start.9
  7.2 4.0 copy-start.8
  7.2 93.7 %reduce-scatter.5.cloned.1.call-start = ((), (), s32[]{:S(2)}) async-start(), calls=%async_computation.4 | async-start | bytes 3342336 | tf_op jit(solution)/shard_map/reduce_scatter | solution.py:72
  9.1 3.4 copy-start.2
  12.5 1.1 copy-start.10
  18.1 0.8 copy-start.3
  18.9 0.6 copy-start.6
  20.6 0.7 copy-start.5
  23.5 3.4 copy-start.11
  33.3 69.5 %copy-start.12 = (f32[3,128]{1,0:T(4,128)S(1)}, f32[3,128]{1,0:T(4,128)}, u32[]{:S(2)}) copy-start(f32[3,128]{1,0:T(4,128)} %get-tuple-element.26) | copy-start | bytes 4612
  33.3 107.6 %all-gather.5.cloned.1.call-start = ((), (), s32[]{:S(2)}) async-start(), calls=%async_computation.5 | async-start | bytes 3342336 | tf_op jit(solution)/shard_map/all_gather | solution.py:78
  102.8 155.7 %reduce-scatter.7.cloned.1.call-start = ((), (), s32[]{:S(2)}) async-start(), calls=%async_computation.6 | async-start | bytes 3342336 | tf_op jit(solution)/shard_map/reduce_scatter | solution.py:72
  102.8 43.9 %copy-start.4 = (bf16[128,384]{0,1:T(8,128)(2,1)S(1)}, bf16[128,384]{0,1:T(8,128)(2,1)}, u32[]{:S(2)}) copy-start(bf16[128,384]{0,1:T(8,128)(2,1)} %copy-done.3) | copy-start | bytes 294916
  102.8 43.9 %copy-start.7 = (pred[128,128]{0,1:T(8,128)(4,1)S(1)}, pred[128,128]{0,1:T(8,128)(4,1)}, u32[]{:S(2)}) copy-start(pred[128,128]{0,1:T(8,128)(4,1)} %copy-done.6) | copy-start | bytes 49156
  190.7 107.5 %all-gather.7.cloned.1.call-start = ((), (), s32[]{:S(2)}) async-start(), calls=%async_computation.7 | async-start | bytes 3342336 | tf_op jit(solution)/shard_map/all_gather | solution.py:78
  260.2 218.5 %reduce-scatter.9.cloned.1.call-start = ((), (), s32[]{:S(2)}) async-start(), calls=%async_computation.8 | async-start | bytes 3342336 | tf_op jit(solution)/shard_map/reduce_scatter | solution.py:72
  419.2 98.7 %all-gather.9.cloned.1.call-start = ((), (), s32[]{:S(2)}) async-start(), calls=%async_computation.9 | async-start | bytes 3342336 | tf_op jit(solution)/shard_map/all_gather | solution.py:78
  480.4 216.9 %reduce-scatter.11.cloned.1.call-start = ((), (), s32[]{:S(2)}) async-start(), calls=%async_computation.10 | async-start | bytes 3342336 | tf_op jit(solution)/shard_map/reduce_scatter | solution.py:72
  637.7 98.9 %all-gather.11.cloned.1.call-start = ((), (), s32[]{:S(2)}) async-start(), calls=%async_computation.11 | async-start | bytes 3342336 | tf_op jit(solution)/shard_map/all_gather | solution.py:78
Sparse Core Ops, SparseCore 0:
  33.4 67.4 reduce-scatter.4
  102.9 37.9 all-gather.4
  190.8 67.6 reduce-scatter.6
  260.3 37.8 all-gather.6
  419.4 59.2 reduce-scatter.8
  480.5 37.4 all-gather.8
  637.8 59.4 reduce-scatter.10
  699.1 37.4 all-gather.10
where the time goes:
time: 826 us; the launch traced here: 825 us
  waiting for transfers between devices  403 us (49%)
  blocking collectives  298 us (36%)
  matrix products  67.5 us (8%)
  between operations  29.8 us (4%)
  other arithmetic  21.9 us (3%)
    reduce_scatter x4, waiting for transfers between devices, head_total(): lax.psum_scatter(partial_value, 'tensor', scatter_dimension=0, tiled=True)  252 us
    all_gather x4, waiting for transfers between devices, head_total(): return lax.all_gather(sent, 'tensor', axis=0, tiled=True)  151 us
    psum x4, blocking collectives, data_sum(): return lax.psum((part[0], part[1]), 'dp')  138 us
    psum x3, blocking collectives, squared(): return lax.psum(local_dot(vector, vector), 'tensor')  89.9 us
    psum x2, blocking collectives, on_device(): curv = lax.psum(local_dot(direction, image), 'tensor')  69.2 us
    dot_general x8, matrix products, attend(): return jnp.dot(mixed, w_out, preferred_element_type=jnp.float32)  39.3 us
  transfers between devices with their start and end apart: 8, of which 8 were waited for; matrix products, arithmetic and copies ran while one was open for 0% of the time, Pallas kernels for 0%

commit v1 on v0

v1 whole, which is shorter than its diff:
```python
import jax
import jax.numpy as jnp
from jax import lax
from jax.experimental import pallas as pl
from jax.experimental.pallas import tpu as pltpu
from jax.sharding import PartitionSpec as P

HEAD_DIM = 128
CG_STEPS = 3
HEADS = 3
COLS = HEADS * HEAD_DIM
ROWS = 128
HALF = ROWS // 2
RANK = 16
WIDTH = 6144
CORE_WIDTH = WIDTH // 2
CHUNKS = CORE_WIDTH // COLS
N_DP = 8
N_Z = 4

EPS = 1e-05
ADAPTER_SCALE = 2.0
DAMP = 0.05
NEG = -1e30

F32 = jnp.float32
BF16 = jnp.bfloat16
MESH = pl.DeviceIdType.MESH

S_W, S_E1, S_S1, S_X1, S_S2, S_Z1, S_X2, S_S3, S_Z2 = 0, 8, 9, 10, 14, 15, 18, 21, 24
S_G, S_S4, S_S5, S_S6, S_E2, S_AR, N_SEND = 25, 39, 42, 43, 44, 45, 52
R_W, R_E1, R_S1, R_X1, R_S2, R_Z1, R_X2, R_S3, R_Z2 = 0, 8, 9, 10, 14, 15, 18, 21, 25
R_G, R_S4, R_S5, R_S6, R_E2, R_AR, N_RECV = 26, 42, 46, 47, 48, 49, 65


def dot(a, b):
    return lax.dot_general(a, b, (((1,), (0,)), ((), ())), preferred_element_type=F32)


def dot_t(a, b):
    return lax.dot_general(a, b, (((1,), (1,)), ((), ())), preferred_element_type=F32)


def split_high_low(x):
    high = x.astype(BF16)
    return high, (x - high.astype(F32)).astype(BF16)


def total(x):
    return jnp.sum(jnp.sum(x, axis=1, keepdims=True), axis=0, keepdims=True)


def kernel(
    len_ref,
    q_ref,
    k_ref,
    v_ref,
    uq_ref,
    uv_ref,
    uqt_ref,
    uvt_ref,
    gap_ref,
    w_ref,
    step_ref,
    remain_ref,
    wb,
    wtmp,
    wsend,
    wrecv,
    pf,
    pb,
    pbt,
    u3,
    ut,
    dmcat,
    e1s,
    e1r,
    part,
    rx1,
    rz1,
    rx2,
    rz2,
    gat,
    cprev,
    cot,
    e2r,
    arb,
    state,
    sca,
    s1r,
    s2r,
    s3b,
    s4b,
    s5r,
    s6r,
    lsem,
    ssem,
    rsem,
):
    d = lax.axis_index("dp")
    t = lax.axis_index("tensor")
    c = lax.rem(t, 2)
    x = lax.rem(t // 2, 2)
    z = t // 4
    sib = (d, t + 1 - 2 * c)
    xn = (d, t + 2 - 4 * x)

    def zn(off):
        return (d, lax.rem(t + 4 * off, 16))

    def dpn(off):
        return (lax.rem(d + off, N_DP), t)

    def remote(src, dst, s, r, device):
        return pltpu.make_async_remote_copy(
            src_ref=src,
            dst_ref=dst,
            send_sem=ssem.at[s],
            recv_sem=rsem.at[r],
            device_id=device,
            device_id_type=MESH,
        )

    barrier = pltpu.get_barrier_semaphore()
    partners = [sib, xn] + [zn(o) for o in (1, 2, 3)] + [dpn(o) for o in range(1, 8)]
    for device in partners:
        pl.semaphore_signal(barrier, inc=1, device_id=device, device_id_type=MESH)

    def own_copy(j):
        columns = pl.ds(pl.multiple_of(c * CORE_WIDTH + j * COLS, COLS), COLS)
        return pltpu.make_async_copy(
            w_ref.at[:, columns], wb.at[j, pl.ds(0, COLS)], lsem.at[j]
        )

    def other_copy(j):
        columns = pl.ds(pl.multiple_of((1 - c) * CORE_WIDTH + j * COLS, COLS), COLS)
        return pltpu.make_async_copy(w_ref.at[:, columns], wtmp.at[j], lsem.at[CHUNKS + j])

    def w_copy(j):
        return remote(wsend.at[j], wrecv.at[j], S_W + j, R_W + j, sib)

    @pl.loop(0, CHUNKS)
    def _(j):
        other_copy(j).start()

    @pl.loop(0, CHUNKS)
    def _(j):
        own_copy(j).start()

    pl.semaphore_wait(barrier, len(partners))

    @pl.loop(0, CHUNKS)
    def _(j):
        other_copy(j).wait()
        wsend[j] = wtmp[j].astype(F32)
        w_copy(j).start()

    limit = len_ref[0]
    row = lax.broadcasted_iota(jnp.int32, (ROWS, ROWS), 0)
    col = lax.broadcasted_iota(jnp.int32, (ROWS, ROWS), 1)
    live = (col <= row) & (col < limit)
    for h in range(HEADS):
        lanes = pl.ds(h * HEAD_DIM, HEAD_DIM)
        scores = dot_t(q_ref[:, lanes], k_ref[:, lanes]) * HEAD_DIM ** (-0.5)
        scores = jnp.where(live, scores, NEG)
        weights = jnp.exp(scores - jnp.max(scores, axis=-1, keepdims=True))
        probs = weights / jnp.sum(weights, axis=-1, keepdims=True)
        pf[h] = probs
        pb[h] = probs.astype(BF16)
        pbt[h] = probs.T.astype(BF16)
        mixed = dot(probs.astype(BF16), v_ref[:, lanes]).astype(BF16)
        dmcat[:, lanes] = mixed
        e1s[h] = mixed.astype(F32)
    for i, ref in enumerate((uq_ref, uv_ref)):
        high, low = split_high_low(ref[...])
        u3[i] = jnp.concatenate([high, high, low], axis=1)
    for i, ref in enumerate((uqt_ref, uvt_ref)):
        high, low = split_high_low(ref[...])
        ut[i] = jnp.concatenate([high, low], axis=0)
    own_rows = lax.broadcasted_iota(jnp.int32, (HALF, COLS), 0) + x * HALF
    mask = (own_rows < limit).astype(F32)
    cprev[0] = gap_ref[0] * mask
    cprev[1] = gap_ref[1] * mask
    state[...] = jnp.zeros_like(state)
    sca[...] = jnp.zeros_like(sca)

    @pl.loop(0, CHUNKS)
    def _(j):
        own_copy(j).wait()
        w_copy(j).wait_recv()
        wb[j, pl.ds(COLS, COLS)] = wrecv[j].astype(BF16)
        w_copy(j).wait_send()

    @pl.loop(0, CG_STEPS + 1)
    def _(k):
        @pl.when(k > 0)
        def _():
            remain = state[0]
            tangents = []
            for i in range(2):
                high, low = split_high_low(remain[i * RANK : (i + 1) * RANK])
                stacked = jnp.concatenate([high, low, high], axis=0)
                tangents.append((ADAPTER_SCALE * dot(u3[i], stacked)).astype(BF16))
            dq, dv = tangents
            for h in range(HEADS):
                lanes = slice(h * HEAD_DIM, (h + 1) * HEAD_DIM)
                scores = dot_t(dq[:, lanes], k_ref[:, lanes]) * HEAD_DIM ** (-0.5)
                probs = pf[h]
                tilted = probs * scores
                dprobs = tilted - probs * jnp.sum(tilted, axis=-1, keepdims=True)
                left = jnp.concatenate([dprobs.astype(BF16), pb[h]], axis=1)
                right = jnp.concatenate([v_ref[:, lanes], dv[:, lanes]], axis=0)
                dmixed = dot(left, right).astype(BF16)
                dmcat[:, lanes] = dmixed
                e1s[h] = dmixed.astype(F32)

        e1 = remote(e1s, e1r, S_E1, R_E1, sib)
        e1.start()
        sca[4] = jnp.broadcast_to(total(state[0] * state[0]), (8, 128))
        s1 = remote(sca.at[4], s1r, S_S1, R_S1, sib)
        s1.start()
        e1.wait_recv()
        for h in range(HEADS):
            dmcat[:, pl.ds(COLS + h * HEAD_DIM, HEAD_DIM)] = e1r[h].astype(BF16)
        s1.wait_recv()
        sca[5] = sca[4] + s1r[...]
        s2 = remote(sca.at[5], s2r, S_S2, R_S2, xn)
        s2.start()

        def x1(zi):
            return remote(part.at[zi, 1 - x], rx1.at[zi], S_X1 + zi, R_X1 + zi, xn)

        def z1(off):
            there = N_Z + lax.rem(z + off, N_Z)
            return remote(part.at[there], rz1.at[off - 1], S_Z1 + off - 1, R_Z1 + off - 1, zn(off))

        @pl.loop(1, N_Z + 1)
        def _(off):
            zi = lax.rem(z + off, N_Z)
            for region in range(2):
                j = zi + region * N_Z
                product = dot(dmcat[...], wb[j])
                part[j, 0] = product[:HALF]
                part[j, 1] = product[HALF:]
                if region == 0:
                    x1(zi).start()
                else:

                    @pl.when(off < N_Z)
                    def _():
                        z1(off).start()

        s2.wait_recv()
        s3b[z] = sca[5] + s2r[...]

        def s3(off):
            return remote(s3b.at[z], s3b.at[z], S_S3 + off - 1, R_S3 + z, zn(off))

        def s3_in(off):
            zi = lax.rem(z + off, N_Z)
            return remote(s3b.at[zi], s3b.at[zi], S_S3 + off - 1, R_S3 + zi, zn(off))

        for off in (1, 2, 3):
            s3(off).start()

        def x2(off):
            there = lax.rem(z + off, N_Z)
            return remote(part.at[there, x], rx2.at[off - 1], S_X2 + off - 1, R_X2 + off - 1, zn(off))

        @pl.loop(1, N_Z + 1)
        def _(off):
            zi = lax.rem(z + off, N_Z)
            x1(zi).wait_recv()
            part[zi, x] = part[zi, x] + rx1[zi]

            @pl.when(off < N_Z)
            def _():
                x2(off).start()

        for off in (1, 2, 3):
            z1(off).wait_recv()
        part[N_Z + z] = part[N_Z + z] + rz1[0] + rz1[1] + rz1[2]
        z2 = remote(part.at[N_Z + z, 1 - x], rz2, S_Z2, R_Z2, xn)
        z2.start()

        for off in (1, 2, 3):
            s3_in(off).wait_recv()
        sca[0] = s3b[0] + s3b[1] + s3b[2] + s3b[3]
        ratio = sca[0] / jnp.where(k > 1, sca[1], 1.0)
        beta = jnp.where(k == 0, 1.0, jnp.where(k == 1, 0.0, ratio))
        beta_row = beta[0:1, 0:1]

        def g_out(half, j, s, device):
            return remote(gat.at[half, j], gat.at[half, j], S_G + s, R_G + half * CHUNKS + j, device)

        for off in (1, 2, 3):
            x2(off).wait_recv()
        cx = part[z, x] + rx2[0] + rx2[1] + rx2[2]
        cx = cx * mask + beta_row * cprev[0]
        cprev[0] = cx
        gat[x, z] = cx
        g_x = [g_out(x, z, off - 1, zn(off)) for off in (1, 2, 3)]
        g_x.append(g_out(x, z, 3, xn))
        for copy in g_x:
            copy.start()
        z2.wait_recv()
        cz = part[N_Z + z, x] + rz2[...]
        cz = cz * mask + beta_row * cprev[1]
        cprev[1] = cz
        gat[x, N_Z + z] = cz
        g_z = [g_out(x, N_Z + z, 7, xn)]
        g_z += [g_out(x, N_Z + z, 7 + off, zn(off)) for off in (1, 2, 3)]
        for copy in g_z:
            copy.start()

        direction = state[0] + beta_row * state[1]
        state[1] = direction
        s4b[z, 0] = jnp.broadcast_to(total(cx * cx) + total(cz * cz), (8, 128))
        s4b[z, 1] = jnp.broadcast_to(total(direction * direction), (8, 128))

        def s4(off):
            return remote(s4b.at[z], s4b.at[z], S_S4 + off - 1, R_S4 + z, zn(off))

        def s4_in(off):
            zi = lax.rem(z + off, N_Z)
            return remote(s4b.at[zi], s4b.at[zi], S_S4 + off - 1, R_S4 + zi, zn(off))

        for off in (1, 2, 3):
            s4(off).start()

        def accumulate(j, first=False):
            both = jnp.concatenate([gat[0, j], gat[1, j]], axis=0).astype(BF16)
            product = dot_t(both, wb[j])
            if first:
                cot[...] = product
            else:
                cot[...] = cot[...] + product

        g_out(1 - x, N_Z + z, 0, xn).wait_recv()
        g_zf = [g_out(1 - x, N_Z + z, 10 + off, zn(off)) for off in (1, 2, 3)]
        for copy in g_zf:
            copy.start()
        accumulate(N_Z + z, first=True)
        g_xf = []
        for off in (1, 3, 2):
            zi = lax.rem(z + off, N_Z)
            g_out(x, zi, 0, xn).wait_recv()
            g_xf.append(g_out(x, zi, 3 + off, xn))
            g_xf[-1].start()
        g_out(1 - x, z, 0, xn).wait_recv()
        accumulate(z)

        for off in (1, 2, 3):
            s4_in(off).wait_recv()
        sca[2] = s4b[0, 0] + s4b[1, 0] + s4b[2, 0] + s4b[3, 0]
        sca[3] = s4b[0, 1] + s4b[1, 1] + s4b[2, 1] + s4b[3, 1]
        s5 = remote(sca.at[pl.ds(2, 2)], s5r, S_S5, R_S5, xn)
        s5.start()

        @pl.loop(1, N_Z)
        def _(off):
            zi = lax.rem(z + off, N_Z)
            g_out(x, N_Z + zi, 0, zn(off)).wait_recv()
            g_out(1 - x, N_Z + zi, 0, zn(off)).wait_recv()
            accumulate(N_Z + zi)
            g_out(1 - x, zi, 0, xn).wait_recv()
            accumulate(zi)

        e2 = remote(cot.at[:, pl.ds(COLS, COLS)], e2r, S_E2, R_E2, sib)
        e2.start()
        s5.wait_recv()
        sca[6] = sca[2] + s5r[0]
        sca[7] = sca[3] + s5r[1]
        s6 = remote(sca.at[pl.ds(6, 2)], s6r, S_S6, R_S6, sib)
        s6.start()
        e2.wait_recv()
        s6.wait_recv()

        parity = lax.rem(k, 2)
        for h in range(HEADS):
            lanes = slice(h * HEAD_DIM, (h + 1) * HEAD_DIM)
            cotan = (cot[:, lanes] + e2r[:, lanes]).astype(BF16)
            dprobs = dot_t(cotan, v_ref[:, lanes])
            probs = pf[h]
            tilted = probs * dprobs
            dscores = tilted - probs * jnp.sum(tilted, axis=-1, keepdims=True)
            dscores = (dscores * HEAD_DIM ** (-0.5)).astype(BF16)
            dq = dot(dscores, k_ref[:, lanes]).astype(BF16)
            dv = dot(pbt[h], cotan).astype(BF16)
            for i, cotangent in enumerate((dq, dv)):
                both = dot(ut[i], cotangent)
                arb[parity, d, i * RANK : (i + 1) * RANK, lanes] = ADAPTER_SCALE * (
                    both[:RANK] + both[RANK:]
                )
        squares = sca[6] + s6r[0]
        for h in range(HEADS):
            arb[parity, d, 2 * RANK : 2 * RANK + 8, h * HEAD_DIM : (h + 1) * HEAD_DIM] = squares

        def ar(off):
            mine = arb.at[parity, d]
            return remote(mine, mine, S_AR + off - 1, R_AR + parity * N_DP + d, dpn(off))

        def ar_in(off):
            peer = lax.rem(d + off, N_DP)
            slot = arb.at[parity, peer]
            return remote(slot, slot, S_AR + off - 1, R_AR + parity * N_DP + peer, dpn(off))

        for off in range(1, N_DP):
            ar(off).start()

        e1.wait_send()
        s1.wait_send()
        s2.wait_send()
        for zi in range(N_Z):
            x1(zi).wait_send()
        for off in (1, 2, 3):
            z1(off).wait_send()
            x2(off).wait_send()
            s3(off).wait_send()
            s4(off).wait_send()
        z2.wait_send()
        for copy in g_x + g_z + g_zf + g_xf:
            copy.wait_send()
        s5.wait_send()
        e2.wait_send()
        s6.wait_send()

        for off in range(1, N_DP):
            ar_in(off).wait_recv()
        for off in range(1, N_DP):
            ar(off).wait_send()
        summed = arb[parity, 0]
        for peer in range(1, N_DP):
            summed = summed + arb[parity, peer]
        summed = summed * (1.0 / (ROWS * N_DP))
        image = summed[: 2 * RANK] + DAMP * state[1]
        squared = summed[2 * RANK :, :HEAD_DIM]
        curvature = squared + DAMP * (sca[7] + s6r[1])
        alpha = jnp.where(k == 0, 1.0, sca[0] / jnp.where(k == 0, 1.0, curvature))[0:1, 0:1]
        state[2] = state[2] + jnp.where(k == 0, 0.0, alpha) * state[1]
        state[0] = state[0] - alpha * image
        sca[1] = sca[0]

    step_ref[...] = state[2]
    remain_ref[...] = state[0]


def solve(lengths, q, k, v, uq, uv, gap, w_out):
    vmem = pl.BlockSpec(memory_space=pltpu.VMEM)
    square = (HEADS, HEAD_DIM, HEAD_DIM)
    block = (HALF, COLS)
    scratch = [
        pltpu.VMEM((CHUNKS, 2 * COLS, COLS), BF16),
        pltpu.VMEM((CHUNKS, COLS, COLS), BF16),
        pltpu.VMEM((CHUNKS, COLS, COLS), F32),
        pltpu.VMEM((CHUNKS, COLS, COLS), F32),
        pltpu.VMEM(square, F32),
        pltpu.VMEM(square, BF16),
        pltpu.VMEM(square, BF16),
        pltpu.VMEM((2, ROWS, 3 * RANK), BF16),
        pltpu.VMEM((2, 2 * RANK, ROWS), BF16),
        pltpu.VMEM((ROWS, 2 * COLS), BF16),
        pltpu.VMEM(square, F32),
        pltpu.VMEM(square, F32),
        pltpu.VMEM((CHUNKS, 2) + block, F32),
        pltpu.VMEM((N_Z,) + block, F32),
        pltpu.VMEM((N_Z - 1, 2) + block, F32),
        pltpu.VMEM((N_Z - 1,) + block, F32),
        pltpu.VMEM(block, F32),
        pltpu.VMEM((2, CHUNKS) + block, F32),
        pltpu.VMEM((2,) + block, F32),
        pltpu.VMEM((ROWS, 2 * COLS), F32),
        pltpu.VMEM((ROWS, COLS), F32),
        pltpu.VMEM((2, N_DP, 2 * RANK + 8, COLS), F32),
        pltpu.VMEM((3, 2 * RANK, COLS), F32),
        pltpu.VMEM((8, 8, 128), F32),
        pltpu.VMEM((8, 128), F32),
        pltpu.VMEM((8, 128), F32),
        pltpu.VMEM((N_Z, 8, 128), F32),
        pltpu.VMEM((N_Z, 2, 8, 128), F32),
        pltpu.VMEM((2, 8, 128), F32),
        pltpu.VMEM((2, 8, 128), F32),
        pltpu.SemaphoreType.DMA((2 * CHUNKS,)),
        pltpu.SemaphoreType.DMA((N_SEND,)),
        pltpu.SemaphoreType.DMA((N_RECV,)),
    ]
    shape = jax.ShapeDtypeStruct((2 * RANK, COLS), F32)
    return pl.pallas_call(
        kernel,
        out_shape=(shape, shape),
        in_specs=[pl.BlockSpec(memory_space=pltpu.SMEM)]
        + [vmem] * 8
        + [pl.BlockSpec(memory_space=pl.ANY)],
        out_specs=(vmem, vmem),
        scratch_shapes=scratch,
        compiler_params=pltpu.CompilerParams(
            collective_id=0, has_side_effects=True, vmem_limit_bytes=48 * 2**20
        ),
        cost_estimate=pl.CostEstimate(
            flops=8 * 2 * ROWS * WIDTH * COLS, bytes_accessed=8 * 2**20, transcendentals=0
        ),
        name="newton",
    )(lengths, q, k, v, uq, uv, uq.T, uv.T, gap, w_out)


def layer_norm(rows, gain, bias):
    rows = rows.astype(F32)
    centred = rows - jnp.mean(rows, axis=-1, keepdims=True)
    spread = jnp.mean(centred * centred, axis=-1, keepdims=True)
    return (centred * lax.rsqrt(spread + EPS) * gain + bias).astype(BF16)


def on_device(
    inputs,
    targets,
    lengths,
    ln_gain,
    ln_bias,
    query_weight,
    w_key,
    value_weight,
    w_out,
    down_query,
    down_value,
    query_up_factor,
    value_up_factor,
):
    normed = layer_norm(inputs, ln_gain, ln_bias)
    downs = jnp.concatenate([down_query, down_value], axis=1)
    both = jnp.dot(normed, downs, preferred_element_type=F32)
    uq, uv = both[:, :RANK], both[:, RANK:]

    def project(weight, low, up):
        rows = jnp.dot(normed, weight, preferred_element_type=F32)
        if up is not None:
            rows = rows + ADAPTER_SCALE * jnp.dot(low, up, precision=lax.Precision.HIGHEST)
        return rows.astype(BF16)

    q = project(query_weight, uq, query_up_factor)
    k = project(w_key, None, None)
    v = project(value_weight, uv, value_up_factor)

    t = lax.axis_index("tensor")
    top = (t // 2) % 2 * HALF
    gaps = []
    for region in range(2):
        left = t % 2 * CORE_WIDTH + region * (CORE_WIDTH // 2) + t // 4 * COLS
        parts = [lax.dynamic_slice(a, (top, left), (HALF, COLS)) for a in (inputs, targets)]
        gaps.append(parts[0].astype(F32) - parts[1].astype(F32))
    gap = jnp.stack(gaps)
    step, remain = solve(lengths, q, k, v, uq, uv, gap, w_out)
    return (step[:RANK], step[RANK:], remain[:RANK], remain[RANK:])


def solution(mesh):
    in_specs = (
        P("dp", None),
        P("dp", None),
        P("dp"),
        P(),
        P(),
        P(None, "tensor"),
        P(None, "tensor"),
        P(None, "tensor"),
        P("tensor", None),
        P(),
        P(),
        P(None, "tensor"),
        P(None, "tensor"),
    )
    out_specs = (P(None, "tensor"), P(None, "tensor"), P(None, "tensor"), P(None, "tensor"))
    return jax.shard_map(
        on_device, mesh=mesh, in_specs=in_specs, out_specs=out_specs, check_vma=False
    )
```

time: 826 us -> 217 us (0.26)
  waiting for transfers between devices: 403 us -> 0 us
  blocking collectives: 298 us -> 0 us
  Pallas kernels: 0 us -> 202 us
  matrix products: 67.5 us -> 4.34 us
  between operations: 29.8 us -> 1.7 us
  other arithmetic: 21.9 us -> 5.39 us
    psum x9 -> x0, blocking collectives: 298 us -> none  [the longest x4 138 us: data_sum(): return lax.psum((part[0], part[1]), 'dp')]
    reduce_scatter x4 -> x0, waiting for transfers between devices: 252 us -> none  [head_total(): lax.psum_scatter(partial_value, 'tensor', scatter_dimension=0, tiled=True)]
    pallas_call x0 -> x1, Pallas kernels: none -> 202 us  [solve(): pl.pallas_call(kernel, out_shape=(shape, shape), in_specs=[pl.BlockSpec(m...]
    all_gather x4 -> x0, waiting for transfers between devices: 151 us -> none  [head_total(): return lax.all_gather(sent, 'tensor', axis=0, tiled=True)]
    dot_general x52 -> x6, matrix products: 67.5 us -> 4.34 us  [the longest x3 2.97 us: project(): rows = jnp.dot(normed, weight, preferred_element_type=F32)]
  transfers between devices with their start and end apart: 8 -> 0, of which waited for: 8 -> 0; matrix products, arithmetic and copies ran while one was open for 0% -> 0% of each run, Pallas kernels for 0% -> 0%
where the time goes in v1:
time: 217 us; the launch traced here: 216 us
  Pallas kernels  202 us (93%)
  other arithmetic  5.39 us (2%)
  matrix products  4.34 us (2%)
  local copies, waits for them, and re-layouts  3.45 us (2%)
    pallas_call x1, Pallas kernels, solve(): pl.pallas_call(kernel, out_shape=(shape, shape), in_specs=[pl.BlockSpec(m...  202 us

profile of v1, /device:TPU:1, one launch (start us, length us, event | category | flops | bytes accessed | tf_op | source)
XLA Modules:
  0.0 216.4 jit_solution(16945227639398140465)
XLA Ops:
  0.6 0.0 copy-start
  0.6 0.0 copy-start.2
  1.5 1.8 convert_reduce_fusion
  3.3 2.0 fusion.2
  5.3 0.0 slice-start
  5.4 0.7 fusion.5
  6.1 0.0 slice-start.1
  6.1 0.0 slice-start.2
  6.1 1.0 fusion.19
  7.1 0.0 slice-start.3
  7.1 0.6 fusion.10
  7.7 0.0 copy-done
  7.8 0.4 fusion.8.q_ref
  8.2 1.0 convolution_convert_fusion.k_ref
  9.2 0.1 slice-done.2
  9.3 0.1 slice-done.3
  9.4 1.0 fusion.20
  10.4 0.4 fusion.9.v_ref
  10.8 0.1 copy.17.uq_ref
  10.9 0.1 copy.18.uv_ref
  11.0 0.9 subtract_bitcast_fusion.1
  11.9 2.3 %copy-done.1 = bf16[384,6144]{1,0:T(8,128)(2,1)S(1)} copy-done((bf16[384,6144]{1,0:T(8,128)(2,1)S(1)}, bf16[384,6144]{1,0:T(8,128)(2,1)}, u32[]{:S(2)}) %copy-start.1) | copy-done | bytes 4718616
  14.2 201.5 %newton.1 = (f32[32,384]{1,0:T(8,128)S(1)}, f32[32,384]{1,0:T(8,128)S(1)}) custom-call(s32[1]{0:T(128)S(6)} %copy.19.len_ref, bf16[128,384]{1,0:T(8,128)(2,1)S(1)} %fusion.8.q_ref, bf16[128,384]{1,0:T(8,128)(2,1)S(1)} %convolution_convert_fusion.k_ref, bf16[128,384]{1,0:T(8,128)(2,1)S(1)} %fusion.9.v_ref, f32[128,16]{1,0:T(8,128)S(1)} %copy.17.uq_ref, ...), custom_call_target="tpu_custom_call" | custom-call | flops 4831838208 | bytes 8388608 | tf_op jit(solution)/shard_map/newton/pallas_call | solution.py:488
  215.8 0.6 fusion.17
  (22 shorter events, 0.1 us)
Async XLA Ops:
  0.6 7.1 %copy-start = (f32[16,384]{1,0:T(8,128)S(1)}, f32[16,384]{1,0:T(8,128)}, u32[]{:S(2)}) copy-start(f32[16,384]{1,0:T(8,128)} %param.24) | copy-start | bytes 73732
  0.6 4.7 %copy-start.2 = (bf16[128,6144]{1,0:T(8,128)(2,1)S(1)}, bf16[128,6144]{1,0:T(8,128)(2,1)}, u32[]{:S(2)}) copy-start(bf16[128,6144]{1,0:T(8,128)(2,1)} %param.13) | copy-start | bytes 4718596
  0.7 4.6 %copy-start.6 = (f32[6144]{0:T(1024)S(1)}, f32[6144]{0:T(1024)}, u32[]{:S(2)}) copy-start(f32[6144]{0:T(1024)} %param.17) | copy-start | bytes 73732
  0.7 4.6 %copy-start.7 = (f32[6144]{0:T(1024)S(1)}, f32[6144]{0:T(1024)}, u32[]{:S(2)}) copy-start(f32[6144]{0:T(1024)} %param.16) | copy-start | bytes 73732
  1.4 4.6 %copy-start.3 = (bf16[6144,384]{1,0:T(8,128)(2,1)S(1)}, bf16[6144,384]{1,0:T(8,128)(2,1)}, u32[]{:S(2)}) copy-start(bf16[6144,384]{1,0:T(8,128)(2,1)} %param.18) | copy-start | bytes 14155780
  5.3 1.8 copy-start.4
  5.3 1.8 copy-start.5
  5.3 2.8 %slice-start = ((s8[4718592]{0:T(1024)(128)(4,1)}), s8[4194304]{0:T(1024)(128)(4,1)S(1)}, s32[]{:S(2)}) async-start(s8[4718592]{0:T(1024)(128)(4,1)} %bitcast.17), calls=%async_computation | async-start | bytes 8388608
  6.1 2.1 slice-start.1
  6.1 3.2 %slice-start.2 = ((s8[4718592]{0:T(1024)(128)(4,1)}), s8[4194304]{0:T(1024)(128)(4,1)S(1)}, s32[]{:S(2)}) async-start(s8[4718592]{0:T(1024)(128)(4,1)} %bitcast.19), calls=%async_computation.2 | async-start | bytes 8388608
  7.1 2.3 %slice-start.3 = ((s8[4718592]{0:T(1024)(128)(4,1)}), s8[524288]{0:T(1024)(128)(4,1)S(1)}, s32[]{:S(2)}) async-start(s8[4718592]{0:T(1024)(128)(4,1)} %bitcast.19), calls=%async_computation.3 | async-start | bytes 1048576
  9.4 1.0 copy-start.8
  11.9 2.3 %copy-start.1 = (bf16[384,6144]{1,0:T(8,128)(2,1)S(1)}, bf16[384,6144]{1,0:T(8,128)(2,1)}, u32[]{:S(2)}) copy-start(bf16[384,6144]{1,0:T(8,128)(2,1)} %w_ref.1) | copy-start | bytes 14155780

commit v2 on v1

v2 whole, which is shorter than its diff:
```python
import jax
import jax.numpy as jnp
from jax import lax
from jax.experimental import pallas as pl
from jax.experimental.pallas import tpu as pltpu
from jax.sharding import PartitionSpec as P

HEAD_DIM = 128
CG_STEPS = 3
HEADS = 3
COLS = HEADS * HEAD_DIM
ROWS = 128
HALF = ROWS // 2
RANK = 16
WIDTH = 6144
CORE_WIDTH = WIDTH // 2
STAGES = 3
LANES = 128
PAIR = 2 * LANES
CHUNKS = CORE_WIDTH // PAIR
N_DP = 8
N_Z = 4

EPS = 1e-05
ADAPTER_SCALE = 2.0
DAMP = 0.05
NEG = -1e30

F32 = jnp.float32
BF16 = jnp.bfloat16
MESH = pl.DeviceIdType.MESH

S_W, S_E1, S_S1, S_S2, S_S3, S_S6, S_E2, S_X1, S_Z1, S_X2 = 0, 12, 15, 16, 17, 20, 21, 22, 25, 34
S_Z2, S_X3, S_X4, S_Z4, S_AR, S_SQ, N_SEND = 43, 46, 55, 58, 67, 74, 81
R_W, R_E1, R_S1, R_S2, R_S3, R_S6, R_E2, R_X1, R_Z1, R_X2 = 0, 12, 15, 16, 17, 21, 22, 23, 26, 35
R_Z2, R_X3, R_X4, R_Z4, R_AR, R_SQ, N_RECV = 44, 47, 59, 62, 74, 90, 106

PEERS = ((1, 2), (1, 1), (1, 3), (0, 2), (1, 0), (0, 1), (0, 3))


def dot(a, b):
    return lax.dot_general(a, b, (((1,), (0,)), ((), ())), preferred_element_type=F32)


def dot_t(a, b):
    return lax.dot_general(a, b, (((1,), (1,)), ((), ())), preferred_element_type=F32)


def split_high_low(x):
    high = x.astype(BF16)
    return high, (x - high.astype(F32)).astype(BF16)


def total(x):
    return jnp.sum(jnp.sum(x, axis=1, keepdims=True), axis=0, keepdims=True)


def kernel(
    len_ref,
    q_ref,
    k_ref,
    v_ref,
    uq_ref,
    uv_ref,
    uqt_ref,
    uvt_ref,
    gap_x_ref,
    gap_z_ref,
    w_ref,
    step_ref,
    remain_ref,
    wb,
    wtmp,
    wsend,
    wrecv,
    pf,
    pb,
    pbt,
    u3,
    ut,
    dmcat,
    e1s,
    e1r,
    part_x,
    part_z,
    rx1,
    rz1,
    rx2,
    rz2,
    gx,
    gz,
    cprev_x,
    cprev_z,
    cot,
    e2r,
    arb,
    sqb,
    squares,
    state,
    sca,
    s1r,
    s2r,
    s3b,
    s6r,
    lsem,
    ssem,
    rsem,
):
    d = lax.axis_index("dp")
    t = lax.axis_index("tensor")
    c = lax.rem(t, 2)
    x = lax.rem(t // 2, 2)
    z = t // 4
    sib = (d, t + 1 - 2 * c)
    xn = (d, t + 2 - 4 * x)

    def zn(off):
        return (d, lax.rem(t + 4 * off, 16))

    def dpn(hop):
        return lax.rem(d // 4 + hop[0], 2) * 4 + lax.rem(d + hop[1], 4)

    def remote(src, dst, s, r, device):
        return pltpu.make_async_remote_copy(
            src_ref=src,
            dst_ref=dst,
            send_sem=ssem.at[s],
            recv_sem=rsem.at[r],
            device_id=device,
            device_id_type=MESH,
        )

    barrier = pltpu.get_barrier_semaphore()
    partners = [sib, xn] + [zn(o) for o in (1, 2, 3)] + [(dpn(hop), t) for hop in PEERS]
    for device in partners:
        pl.semaphore_signal(barrier, inc=1, device_id=device, device_id_type=MESH)

    def own_copy(j):
        columns = pl.ds(pl.multiple_of(c * CORE_WIDTH + j * PAIR, PAIR), PAIR)
        return pltpu.make_async_copy(
            w_ref.at[:, columns], wb.at[j, pl.ds(0, COLS)], lsem.at[j]
        )

    def other_copy(j):
        columns = pl.ds(pl.multiple_of((1 - c) * CORE_WIDTH + j * PAIR, PAIR), PAIR)
        return pltpu.make_async_copy(w_ref.at[:, columns], wtmp.at[j], lsem.at[CHUNKS + j])

    def w_copy(j):
        return remote(wsend.at[j], wrecv.at[j], S_W + j, R_W + j, sib)

    @pl.loop(0, CHUNKS)
    def _(j):
        other_copy(j).start()

    @pl.loop(0, CHUNKS)
    def _(j):
        own_copy(j).start()

    pl.semaphore_wait(barrier, len(partners))

    @pl.loop(0, CHUNKS)
    def _(j):
        other_copy(j).wait()
        wsend[j] = wtmp[j].astype(F32)
        w_copy(j).start()

    limit = len_ref[0]
    row = lax.broadcasted_iota(jnp.int32, (ROWS, ROWS), 0)
    col = lax.broadcasted_iota(jnp.int32, (ROWS, ROWS), 1)
    live = (col <= row) & (col < limit)
    for h in range(HEADS):
        lanes = pl.ds(h * HEAD_DIM, HEAD_DIM)
        scores = dot_t(q_ref[:, lanes], k_ref[:, lanes]) * HEAD_DIM ** (-0.5)
        scores = jnp.where(live, scores, NEG)
        weights = jnp.exp(scores - jnp.max(scores, axis=-1, keepdims=True))
        probs = weights / jnp.sum(weights, axis=-1, keepdims=True)
        pf[h] = probs
        pb[h] = probs.astype(BF16)
        pbt[h] = probs.T.astype(BF16)
        mixed = dot(probs.astype(BF16), v_ref[:, lanes]).astype(BF16)
        dmcat[:, lanes] = mixed
        e1s[h] = mixed.astype(F32)
    for i, ref in enumerate((uq_ref, uv_ref)):
        high, low = split_high_low(ref[...])
        u3[i] = jnp.concatenate([high, high, low], axis=1)
    for i, ref in enumerate((uqt_ref, uvt_ref)):
        high, low = split_high_low(ref[...])
        ut[i] = jnp.concatenate([high, low], axis=0)
    place = lax.broadcasted_iota(jnp.int32, (ROWS, LANES), 0)
    mask_z = (place < limit).astype(F32)
    mask_x = (place[:HALF] + x * HALF < limit).astype(F32)
    for s in range(STAGES):
        cprev_x[s] = gap_x_ref[s] * mask_x
        cprev_z[s] = gap_z_ref[s] * mask_z
    state[...] = jnp.zeros_like(state)
    sca[...] = jnp.zeros_like(sca)

    @pl.loop(0, CHUNKS)
    def _(j):
        own_copy(j).wait()
        w_copy(j).wait_recv()
        wb[j, pl.ds(COLS, COLS)] = wrecv[j].astype(BF16)
        w_copy(j).wait_send()

    @pl.loop(0, CG_STEPS + 1)
    def _(k):
        def e1(h):
            return remote(e1s.at[h], e1r.at[h], S_E1 + h, R_E1 + h, sib)

        @pl.when(k > 0)
        def _():
            remain = state[0]
            tangents = []
            for i in range(2):
                high, low = split_high_low(remain[i * RANK : (i + 1) * RANK])
                stacked = jnp.concatenate([high, low, high], axis=0)
                tangents.append((ADAPTER_SCALE * dot(u3[i], stacked)).astype(BF16))
            dq, dv = tangents
            for h in range(HEADS):
                lanes = slice(h * HEAD_DIM, (h + 1) * HEAD_DIM)
                scores = dot_t(dq[:, lanes], k_ref[:, lanes]) * HEAD_DIM ** (-0.5)
                probs = pf[h]
                tilted = probs * scores
                dprobs = tilted - probs * jnp.sum(tilted, axis=-1, keepdims=True)
                left = jnp.concatenate([dprobs.astype(BF16), pb[h]], axis=1)
                right = jnp.concatenate([v_ref[:, lanes], dv[:, lanes]], axis=0)
                dmixed = dot(left, right).astype(BF16)
                dmcat[:, lanes] = dmixed
                e1s[h] = dmixed.astype(F32)
                e1(h).start()

        @pl.when(k == 0)
        def _():
            for h in range(HEADS):
                e1(h).start()

        sca[4] = jnp.broadcast_to(total(state[0] * state[0]), (8, 128))
        sca[5] = jnp.broadcast_to(total(state[0] * state[1]), (8, 128))
        s1 = remote(sca.at[pl.ds(4, 2)], s1r, S_S1, R_S1, sib)
        s1.start()
        for h in range(HEADS):
            e1(h).wait_recv()
            dmcat[:, pl.ds(COLS + h * HEAD_DIM, HEAD_DIM)] = e1r[h].astype(BF16)
        s1.wait_recv()
        sca[pl.ds(6, 2)] = sca[pl.ds(4, 2)] + s1r[...]
        s2 = remote(sca.at[pl.ds(6, 2)], s2r, S_S2, R_S2, xn)
        s2.start()

        def zi(off):
            return lax.rem(z + off, N_Z)

        def x1(s):
            return remote(part_x.at[s, 1 - x], rx1.at[s], S_X1 + s, R_X1 + s, xn)

        def z1(s, off):
            i = 3 * s + off - 1
            return remote(part_z.at[s, zi(off)], rz1.at[s, off - 1], S_Z1 + i, R_Z1 + i, zn(off))

        def x2(s, off):
            i = 3 * s + off - 1
            return remote(part_x.at[s, x, zi(off)], rx2.at[s, off - 1], S_X2 + i, R_X2 + i, zn(off))

        def z2(s):
            return remote(part_z.at[s, z], rz2.at[s], S_Z2 + s, R_Z2 + s, xn)

        for s in range(STAGES):
            for off in (2, 1, 3, 0):
                product = dot(dmcat[...], wb[s * N_Z + zi(off)])
                part_z[s, zi(off)] = product[:, LANES:]
                if off:
                    z1(s, off).start()
                part_x[s, 0, zi(off)] = product[:HALF, :LANES]
                part_x[s, 1, zi(off)] = product[HALF:, :LANES]
            x1(s).start()

        s2.wait_recv()
        s3b[z] = sca[pl.ds(6, 2)] + s2r[...]

        def s3(off, peer):
            return remote(s3b.at[peer], s3b.at[peer], S_S3 + off - 1, R_S3 + peer, zn(off))

        for off in (2, 1, 3):
            s3(off, z).start()

        for s in range(STAGES):
            x1(s).wait_recv()
            part_x[s, x] = part_x[s, x] + rx1[s]
            for off in (2, 1, 3):
                x2(s, off).start()
            for off in (1, 2, 3):
                z1(s, off).wait_recv()
            part_z[s, z] = part_z[s, z] + rz1[s, 0] + rz1[s, 1] + rz1[s, 2]
            z2(s).start()

        for off in (1, 2, 3):
            s3(off, zi(off)).wait_recv()
        sums = s3b[0] + s3b[1] + s3b[2] + s3b[3]
        sca[0] = sums[0]
        ratio = sums[0] / jnp.where(k > 1, sca[1], 1.0)
        beta = jnp.where(k == 0, 1.0, jnp.where(k == 1, 0.0, ratio))
        beta_row = beta[0:1, 0:1]
        sca[2] = sums[0] + 2.0 * beta * sums[1] + beta * beta * sca[2]

        def x3(s, off, peer):
            block = gx.at[s, x, peer]
            return remote(block, block, S_X3 + 3 * s + off - 1, R_X3 + N_Z * s + peer, zn(off))

        def x4(s, half):
            return remote(gx.at[s, half], gx.at[s, half], S_X4 + s, R_X4 + s, xn)

        def z4(s, off, peer):
            block = gz.at[s, peer]
            return remote(block, block, S_Z4 + 3 * s + off - 1, R_Z4 + N_Z * s + peer, zn(off))

        def own_x(s):
            for off in (1, 2, 3):
                x2(s, off).wait_recv()
            block = part_x[s, x, z] + rx2[s, 0] + rx2[s, 1] + rx2[s, 2]
            block = block * mask_x + beta_row * cprev_x[s]
            cprev_x[s] = block
            gx[s, x, z] = block
            for off in (2, 1, 3):
                x3(s, off, z).start()

        def own_z(s):
            z2(s).wait_recv()
            block = part_z[s, z] + rz2[s]
            block = block * mask_z + beta_row * cprev_z[s]
            cprev_z[s] = block
            gz[s, z] = block
            for off in (2, 1, 3):
                z4(s, off, z).start()

        own_x(0)
        own_x(1)
        own_z(0)
        own_x(2)
        own_z(1)
        own_z(2)
        state[1] = state[0] + beta_row * state[1]
        for s in range(STAGES):
            for off in (1, 3, 2):
                x3(s, off, zi(off)).wait_recv()
            x4(s, x).start()

        squares[...] = jnp.zeros_like(squares)
        for s in range(STAGES):
            x4(s, 1 - x).wait_recv()
            for off in (0, 1, 3, 2):
                if off:
                    z4(s, off, zi(off)).wait_recv()
                left = jnp.concatenate([gx[s, 0, zi(off)], gx[s, 1, zi(off)]], axis=0)
                both = jnp.concatenate([left, gz[s, zi(off)]], axis=1)
                product = dot_t(both.astype(BF16), wb[s * N_Z + zi(off)])
                if s == 0 and off == 0:
                    cot[...] = product
                else:
                    cot[...] = cot[...] + product
                squares[...] = squares[...] + both * both

        e2 = remote(cot.at[:, pl.ds(COLS, COLS)], e2r, S_E2, R_E2, sib)
        e2.start()
        sca[3] = jnp.broadcast_to(total(squares[...]), (8, 128))
        s6 = remote(sca.at[3], s6r, S_S6, R_S6, sib)
        s6.start()
        s6.wait_recv()

        parity = lax.rem(k, 2)

        def ar(i, peer):
            block = arb.at[parity, peer]
            r = R_AR + parity * N_DP + peer
            return remote(block, block, S_AR + i, r, (dpn(PEERS[i]), t))

        def sq(i, peer):
            block = sqb.at[parity, peer]
            r = R_SQ + parity * N_DP + peer
            return remote(block, block, S_SQ + i, r, (dpn(PEERS[i]), t))

        sqb[parity, d] = sca[3] + s6r[...]
        for i in range(N_DP - 1):
            sq(i, d).start()
        e2.wait_recv()
        for h in range(HEADS):
            lanes = slice(h * HEAD_DIM, (h + 1) * HEAD_DIM)
            cotan = (cot[:, lanes] + e2r[:, lanes]).astype(BF16)
            dprobs = dot_t(cotan, v_ref[:, lanes])
            probs = pf[h]
            tilted = probs * dprobs
            dscores = tilted - probs * jnp.sum(tilted, axis=-1, keepdims=True)
            dscores = (dscores * HEAD_DIM ** (-0.5)).astype(BF16)
            dq = dot(dscores, k_ref[:, lanes]).astype(BF16)
            dv = dot(pbt[h], cotan).astype(BF16)
            for i, cotangent in enumerate((dq, dv)):
                both = dot(ut[i], cotangent)
                arb[parity, d, i * RANK : (i + 1) * RANK, lanes] = ADAPTER_SCALE * (
                    both[:RANK] + both[RANK:]
                )
        for i in range(N_DP - 1):
            ar(i, d).start()

        for h in range(HEADS):
            e1(h).wait_send()
        s1.wait_send()
        s2.wait_send()
        for off in (1, 2, 3):
            s3(off, z).wait_send()
        for s in range(STAGES):
            x1(s).wait_send()
            z2(s).wait_send()
            x4(s, x).wait_send()
            for off in (1, 2, 3):
                z1(s, off).wait_send()
                x2(s, off).wait_send()
                x3(s, off, z).wait_send()
                z4(s, off, z).wait_send()
        e2.wait_send()
        s6.wait_send()

        for i in reversed(range(N_DP - 1)):
            ar(i, dpn(PEERS[i])).wait_recv()
            sq(i, dpn(PEERS[i])).wait_recv()
        for i in range(N_DP - 1):
            ar(i, d).wait_send()
            sq(i, d).wait_send()
        summed = arb[parity, 0]
        for peer in range(1, N_DP):
            summed = summed + arb[parity, peer]
        image = summed * (1.0 / (ROWS * N_DP)) + DAMP * state[1]
        squared = sqb[parity, 0]
        for peer in range(1, N_DP):
            squared = squared + sqb[parity, peer]
        squared = squared * (1.0 / (ROWS * N_DP))
        curvature = squared + DAMP * sca[2]
        alpha = jnp.where(k == 0, 1.0, sca[0] / jnp.where(k == 0, 1.0, curvature))[0:1, 0:1]
        state[2] = state[2] + jnp.where(k == 0, 0.0, alpha) * state[1]
        state[0] = state[0] - alpha * image
        sca[1] = sca[0]

    step_ref[...] = state[2]
    remain_ref[...] = state[0]


def solve(lengths, q, k, v, uq, uv, gap_x, gap_z, w_out):
    vmem = pl.BlockSpec(memory_space=pltpu.VMEM)
    square = (HEADS, HEAD_DIM, HEAD_DIM)
    half_block = (HALF, LANES)
    block = (ROWS, LANES)
    scratch = [
        pltpu.VMEM((CHUNKS, 2 * COLS, PAIR), BF16),
        pltpu.VMEM((CHUNKS, COLS, PAIR), BF16),
        pltpu.VMEM((CHUNKS, COLS, PAIR), F32),
        pltpu.VMEM((CHUNKS, COLS, PAIR), F32),
        pltpu.VMEM(square, F32),
        pltpu.VMEM(square, BF16),
        pltpu.VMEM(square, BF16),
        pltpu.VMEM((2, ROWS, 3 * RANK), BF16),
        pltpu.VMEM((2, 2 * RANK, ROWS), BF16),
        pltpu.VMEM((ROWS, 2 * COLS), BF16),
        pltpu.VMEM(square, F32),
        pltpu.VMEM(square, F32),
        pltpu.VMEM((STAGES, 2, N_Z) + half_block, F32),
        pltpu.VMEM((STAGES, N_Z) + block, F32),
        pltpu.VMEM((STAGES, N_Z) + half_block, F32),
        pltpu.VMEM((STAGES, N_Z - 1) + block, F32),
        pltpu.VMEM((STAGES, N_Z - 1) + half_block, F32),
        pltpu.VMEM((STAGES,) + block, F32),
        pltpu.VMEM((STAGES, 2, N_Z) + half_block, F32),
        pltpu.VMEM((STAGES, N_Z) + block, F32),
        pltpu.VMEM((STAGES,) + half_block, F32),
        pltpu.VMEM((STAGES,) + block, F32),
        pltpu.VMEM((ROWS, 2 * COLS), F32),
        pltpu.VMEM((ROWS, COLS), F32),
        pltpu.VMEM((2, N_DP, 2 * RANK, COLS), F32),
        pltpu.VMEM((2, N_DP, 8, 128), F32),
        pltpu.VMEM((ROWS, PAIR), F32),
        pltpu.VMEM((3, 2 * RANK, COLS), F32),
        pltpu.VMEM((8, 8, 128), F32),
        pltpu.VMEM((2, 8, 128), F32),
        pltpu.VMEM((2, 8, 128), F32),
        pltpu.VMEM((N_Z, 2, 8, 128), F32),
        pltpu.VMEM((8, 128), F32),
        pltpu.SemaphoreType.DMA((2 * CHUNKS,)),
        pltpu.SemaphoreType.DMA((N_SEND,)),
        pltpu.SemaphoreType.DMA((N_RECV,)),
    ]
    shape = jax.ShapeDtypeStruct((2 * RANK, COLS), F32)
    return pl.pallas_call(
        kernel,
        out_shape=(shape, shape),
        in_specs=[pl.BlockSpec(memory_space=pltpu.SMEM)]
        + [vmem] * 9
        + [pl.BlockSpec(memory_space=pl.ANY)],
        out_specs=(vmem, vmem),
        scratch_shapes=scratch,
        compiler_params=pltpu.CompilerParams(
            collective_id=0, has_side_effects=True, vmem_limit_bytes=48 * 2**20
        ),
        cost_estimate=pl.CostEstimate(
            flops=8 * 2 * ROWS * WIDTH * COLS, bytes_accessed=8 * 2**20, transcendentals=0
        ),
        name="newton",
    )(lengths, q, k, v, uq, uv, uq.T, uv.T, gap_x, gap_z, w_out)


def layer_norm(rows, gain, bias):
    rows = rows.astype(F32)
    centred = rows - jnp.mean(rows, axis=-1, keepdims=True)
    spread = jnp.mean(centred * centred, axis=-1, keepdims=True)
    return (centred * lax.rsqrt(spread + EPS) * gain + bias).astype(BF16)


def on_device(
    inputs,
    targets,
    lengths,
    ln_gain,
    ln_bias,
    query_weight,
    w_key,
    value_weight,
    w_out,
    down_query,
    down_value,
    query_up_factor,
    value_up_factor,
):
    normed = layer_norm(inputs, ln_gain, ln_bias)
    downs = jnp.concatenate([down_query, down_value], axis=1)
    both = jnp.dot(normed, downs, preferred_element_type=F32)
    uq, uv = both[:, :RANK], both[:, RANK:]

    def project(weight, low, up):
        rows = jnp.dot(normed, weight, preferred_element_type=F32)
        if up is not None:
            rows = rows + ADAPTER_SCALE * jnp.dot(low, up, precision=lax.Precision.HIGHEST)
        return rows.astype(BF16)

    q = project(query_weight, uq, query_up_factor)
    k = project(w_key, None, None)
    v = project(value_weight, uv, value_up_factor)

    t = lax.axis_index("tensor")
    gaps_x, gaps_z = [], []
    for s in range(STAGES):
        left = t % 2 * CORE_WIDTH + (s * N_Z + t // 4) * PAIR
        top = (t // 2) % 2 * HALF
        for gaps, size, at in (
            (gaps_x, (HALF, LANES), (top, left)),
            (gaps_z, (ROWS, LANES), (0, left + LANES)),
        ):
            parts = [lax.dynamic_slice(a, at, size) for a in (inputs, targets)]
            gaps.append(parts[0].astype(F32) - parts[1].astype(F32))
    step, remain = solve(lengths, q, k, v, uq, uv, jnp.stack(gaps_x), jnp.stack(gaps_z), w_out)
    return (step[:RANK], step[RANK:], remain[:RANK], remain[RANK:])


def solution(mesh):
    in_specs = (
        P("dp", None),
        P("dp", None),
        P("dp"),
        P(),
        P(),
        P(None, "tensor"),
        P(None, "tensor"),
        P(None, "tensor"),
        P("tensor", None),
        P(),
        P(),
        P(None, "tensor"),
        P(None, "tensor"),
    )
    out_specs = (P(None, "tensor"), P(None, "tensor"), P(None, "tensor"), P(None, "tensor"))
    return jax.shard_map(
        on_device, mesh=mesh, in_specs=in_specs, out_specs=out_specs, check_vma=False
    )
```

time: 217 us -> 197 us (0.908)
  Pallas kernels: 202 us -> 181 us
    pallas_call x1, Pallas kernels: 202 us -> 181 us  [solve(): pl.pallas_call(kernel, out_shape=(shape, shape), in_specs=[pl.BlockSpec(m...]
where the time goes in v2:
time: 197 us
  Pallas kernels  181 us (92%)
  other arithmetic  6.16 us (3%)
  matrix products  4.34 us (2%)
  local copies, waits for them, and re-layouts  3.45 us (2%)
    pallas_call x1, Pallas kernels, solve(): pl.pallas_call(kernel, out_shape=(shape, shape), in_specs=[pl.BlockSpec(m...  181 us

profile of v2, /device:TPU:1, one launch (start us, length us, event | category | flops | bytes accessed | tf_op | source)
XLA Modules:
  0.0 197.1 jit_solution(15008206944526635160)
XLA Ops:
  0.6 0.0 copy-start
  1.5 1.8 convert_reduce_fusion
  3.3 2.0 %fusion.2 = f32[128]{0:T(128)S(1)} fusion(bf16[128,6144]{1,0:T(8,128)(2,1)} %param.13, f32[128]{0:T(128)S(1)} %broadcast_multiply_fusion), kind=kLoop, calls=%fused_computation.4 | loop fusion | flops 3145600 | bytes 1573888 | tf_op jit(solution)/shard_map/reduce_sum | solution.py:509
  5.3 0.0 slice-start
  5.4 0.7 fusion.5
  6.1 0.0 slice-start.1
  6.1 0.0 slice-start.2
  6.1 1.0 fusion.19
  7.1 0.0 slice-start.3
  7.1 0.6 fusion.10
  7.7 0.0 copy-done
  7.8 0.4 fusion.8.q_ref
  8.2 1.0 convolution_convert_fusion.k_ref
  9.2 0.1 slice-done.2
  9.3 0.1 slice-done.3
  9.4 1.0 fusion.20
  10.4 0.4 fusion.9.v_ref
  10.8 0.1 copy.17.uq_ref
  10.9 0.1 copy.18.uv_ref
  11.0 0.8 subtract_bitcast_fusion.5
  11.8 0.8 subtract_bitcast_fusion.2
  12.7 2.3 %copy-done.1 = bf16[384,6144]{1,0:T(8,128)(2,1)S(1)} copy-done((bf16[384,6144]{1,0:T(8,128)(2,1)S(1)}, bf16[384,6144]{1,0:T(8,128)(2,1)}, u32[]{:S(2)}) %copy-start.1) | copy-done | bytes 4718616
  15.0 181.4 %newton.1 = (f32[32,384]{1,0:T(8,128)S(1)}, f32[32,384]{1,0:T(8,128)S(1)}) custom-call(s32[1]{0:T(128)S(6)} %copy.19.len_ref, bf16[128,384]{1,0:T(8,128)(2,1)S(1)} %fusion.8.q_ref, bf16[128,384]{1,0:T(8,128)(2,1)S(1)} %convolution_convert_fusion.k_ref, bf16[128,384]{1,0:T(8,128)(2,1)S(1)} %fusion.9.v_ref, f32[128,16]{1,0:T(8,128)S(1)} %copy.17.uq_ref, ...), custom_call_target="tpu_custom_call" | custom-call | flops 4831838208 | bytes 8388608 | tf_op jit(solution)/shard_map/newton/pallas_call | solution.py:488
  196.5 0.6 fusion.17
  (24 shorter events, 0.1 us)
Async XLA Ops:
  0.6 7.1 %copy-start = (f32[16,384]{1,0:T(8,128)S(1)}, f32[16,384]{1,0:T(8,128)}, u32[]{:S(2)}) copy-start(f32[16,384]{1,0:T(8,128)} %param.24) | copy-start | bytes 73732
  0.6 4.7 %copy-start.2 = (bf16[128,6144]{1,0:T(8,128)(2,1)S(1)}, bf16[128,6144]{1,0:T(8,128)(2,1)}, u32[]{:S(2)}) copy-start(bf16[128,6144]{1,0:T(8,128)(2,1)} %param.13) | copy-start | bytes 4718596
  0.7 4.6 %copy-start.6 = (f32[6144]{0:T(1024)S(1)}, f32[6144]{0:T(1024)}, u32[]{:S(2)}) copy-start(f32[6144]{0:T(1024)} %param.17) | copy-start | bytes 73732
  0.7 4.6 %copy-start.7 = (f32[6144]{0:T(1024)S(1)}, f32[6144]{0:T(1024)}, u32[]{:S(2)}) copy-start(f32[6144]{0:T(1024)} %param.16) | copy-start | bytes 73732
  1.4 4.6 %copy-start.3 = (bf16[6144,384]{1,0:T(8,128)(2,1)S(1)}, bf16[6144,384]{1,0:T(8,128)(2,1)}, u32[]{:S(2)}) copy-start(bf16[6144,384]{1,0:T(8,128)(2,1)} %param.18) | copy-start | bytes 14155780
  5.3 1.8 copy-start.4
  5.3 1.8 copy-start.5
  5.3 2.8 %slice-start = ((s8[4718592]{0:T(1024)(128)(4,1)}), s8[4194304]{0:T(1024)(128)(4,1)S(1)}, s32[]{:S(2)}) async-start(s8[4718592]{0:T(1024)(128)(4,1)} %bitcast.25), calls=%async_computation | async-start | bytes 8388608
  6.1 2.1 %slice-start.1 = ((s8[4718592]{0:T(1024)(128)(4,1)}), s8[524288]{0:T(1024)(128)(4,1)S(1)}, s32[]{:S(2)}) async-start(s8[4718592]{0:T(1024)(128)(4,1)} %bitcast.25), calls=%async_computation.1 | async-start | bytes 1048576
  6.1 3.2 %slice-start.2 = ((s8[4718592]{0:T(1024)(128)(4,1)}), s8[4194304]{0:T(1024)(128)(4,1)S(1)}, s32[]{:S(2)}) async-start(s8[4718592]{0:T(1024)(128)(4,1)} %bitcast.27), calls=%async_computation.2 | async-start | bytes 8388608
  7.1 2.3 %slice-start.3 = ((s8[4718592]{0:T(1024)(128)(4,1)}), s8[524288]{0:T(1024)(128)(4,1)S(1)}, s32[]{:S(2)}) async-start(s8[4718592]{0:T(1024)(128)(4,1)} %bitcast.27), calls=%async_computation.3 | async-start | bytes 1048576
  9.4 1.0 copy-start.8
  12.7 2.3 %copy-start.1 = (bf16[384,6144]{1,0:T(8,128)(2,1)S(1)}, bf16[384,6144]{1,0:T(8,128)(2,1)}, u32[]{:S(2)}) copy-start(bf16[384,6144]{1,0:T(8,128)(2,1)} %w_ref.1) | copy-start | bytes 14155780

commit v3 on v2

--- a/solution.py
+++ b/solution.py
@@ -20,6 +20,7 @@
 CHUNKS = CORE_WIDTH // PAIR
 N_DP = 8
 N_Z = 4
+DEPTH = 768
 
 EPS = 1e-05
 ADAPTER_SCALE = 2.0
@@ -30,10 +31,10 @@
 BF16 = jnp.bfloat16
 MESH = pl.DeviceIdType.MESH
 
-S_W, S_E1, S_S1, S_S2, S_S3, S_S6, S_E2, S_X1, S_Z1, S_X2 = 0, 12, 15, 16, 17, 20, 21, 22, 25, 34
-S_Z2, S_X3, S_X4, S_Z4, S_AR, S_SQ, N_SEND = 43, 46, 55, 58, 67, 74, 81
-R_W, R_E1, R_S1, R_S2, R_S3, R_S6, R_E2, R_X1, R_Z1, R_X2 = 0, 12, 15, 16, 17, 21, 22, 23, 26, 35
-R_Z2, R_X3, R_X4, R_Z4, R_AR, R_SQ, N_RECV = 44, 47, 59, 62, 74, 90, 106
+S_W, S_E1, S_S1, S_S2, S_S3, S_S6, S_E2, S_X1, S_Z1, S_X2 = 0, 12, 15, 16, 17, 20, 21, 22, 25, 43
+S_Z2, S_X3, S_X4, S_Z4, S_AR, S_SQ, N_SEND = 52, 55, 64, 76, 88, 95, 102
+R_W, R_E1, R_S1, R_S2, R_S3, R_S6, R_E2, R_X1, R_Z1, R_X2 = 0, 12, 15, 16, 17, 21, 22, 23, 26, 44
+R_Z2, R_X3, R_X4, R_Z4, R_AR, R_SQ, N_RECV = 53, 56, 68, 80, 92, 108, 124
 
 PEERS = ((1, 2), (1, 1), (1, 3), (0, 2), (1, 0), (0, 1), (0, 3))
 
@@ -57,18 +58,30 @@
 
 def kernel(
     len_ref,
+    gain_ref,
+    bias_ref,
+    bq_ref,
+    bv_ref,
+    inputs_ref,
+    targets_ref,
+    wq_ref,
+    wk_ref,
+    wv_ref,
+    dq_ref,
+    dv_ref,
+    w_ref,
+    step_ref,
+    remain_ref,
+    inputs_v,
+    targets_x,
+    targets_z,
+    normed,
+    weights_v,
+    rows_v,
+    down_v,
     q_ref,
     k_ref,
     v_ref,
-    uq_ref,
-    uv_ref,
-    uqt_ref,
-    uvt_ref,
-    gap_x_ref,
-    gap_z_ref,
-    w_ref,
-    step_ref,
-    remain_ref,
     wb,
     wtmp,
     wsend,
@@ -84,6 +97,7 @@
     part_x,
     part_z,
     rx1,
+    rz0,
     rz1,
     rx2,
     rz2,
@@ -103,6 +117,7 @@
     s3b,
     s6r,
     lsem,
+    psem,
     ssem,
     rsem,
 ):
@@ -148,21 +163,114 @@
     def w_copy(j):
         return remote(wsend.at[j], wrecv.at[j], S_W + j, R_W + j, sib)
 
+    def order(i):
+        return i // N_Z * N_Z + lax.rem(z + lax.rem(i + 2, N_Z), N_Z)
+
+    def load(source, target, pieces, first):
+        rows = source.shape[0] // pieces
+        return [
+            pltpu.make_async_copy(
+                source.at[pl.ds(i * rows, rows)], target.at[pl.ds(i * rows, rows)], psem.at[first + i]
+            )
+            for i in range(pieces)
+        ]
+
+    load_inputs = load(inputs_ref, inputs_v, 4, 0)
+    load_downs = [
+        pltpu.make_async_copy(ref, down_v.at[pl.ds(i * RANK, RANK)], psem.at[4 + i])
+        for i, ref in enumerate((dq_ref, dv_ref))
+    ]
+    half_rows = pl.ds(pl.multiple_of(x * HALF, HALF), HALF)
+
+    def gap_lanes(s, region):
+        left = c * CORE_WIDTH + (s * N_Z + z) * PAIR + region * LANES
+        return pl.ds(pl.multiple_of(left, LANES), LANES)
+
+    load_targets = []
+    for s in range(STAGES):
+        for i, (rows, target) in enumerate(((half_rows, targets_x), (pl.ds(0, ROWS), targets_z))):
+            source = targets_ref.at[rows, gap_lanes(s, i)]
+            load_targets.append(
+                pltpu.make_async_copy(source, target.at[s], psem.at[6 + 2 * s + i])
+            )
+
+    def load_weights(i):
+        rows = pl.ds(i * DEPTH, DEPTH)
+        return [
+            pltpu.make_async_copy(
+                ref.at[rows],
+                weights_v.at[rows, pl.ds(n * COLS, COLS)],
+                psem.at[12 + 3 * i + n],
+            )
+            for n, ref in enumerate((wq_ref, wk_ref, wv_ref))
+        ]
+
+    pieces = [load_weights(i) for i in range(WIDTH // DEPTH)]
+    for copy in load_inputs:
+        copy.start()
+
     @pl.loop(0, CHUNKS)
-    def _(j):
-        other_copy(j).start()
+    def _(i):
+        other_copy(order(i)).start()
+
+    for copy in load_downs + sum(pieces[:4], []):
+        copy.start()
+
+    for i, copy in enumerate(load_inputs):
+        copy.wait()
+        if i < 2:
+            for late in pieces[4 + 2 * i] + pieces[5 + 2 * i]:
+                late.start()
+        if i == 2:
+
+            @pl.loop(0, CHUNKS)
+            def _(j):
+                own_copy(order(j)).start()
+
+            for late in load_targets:
+                late.start()
+
+        size = ROWS // len(load_inputs)
+
+        @pl.loop(i * size // 16, (i + 1) * size // 16)
+        def _(r):
+            rows = pl.ds(pl.multiple_of(r * 16, 16), 16)
+            wide = inputs_v[rows, :].astype(F32)
+            centred = wide - jnp.sum(wide, axis=1, keepdims=True) * (1.0 / WIDTH)
+            spread = jnp.sum(centred * centred, axis=1, keepdims=True) * (1.0 / WIDTH)
+            scaled = centred * lax.rsqrt(spread + EPS)
+            normed[rows, :] = (scaled * gain_ref[...] + bias_ref[...]).astype(BF16)
+
+    pl.semaphore_wait(barrier, len(partners))
 
     @pl.loop(0, CHUNKS)
-    def _(j):
-        own_copy(j).start()
-
-    pl.semaphore_wait(barrier, len(partners))
-
-    @pl.loop(0, CHUNKS)
-    def _(j):
+    def _(i):
+        j = order(i)
         other_copy(j).wait()
         wsend[j] = wtmp[j].astype(F32)
         w_copy(j).start()
+
+    for i, piece in enumerate(pieces):
+        for copy in piece:
+            copy.wait()
+        depth = pl.ds(i * DEPTH, DEPTH)
+        product = dot(normed[:, depth], weights_v[depth, :])
+        rows_v[...] = product if i == 0 else rows_v[...] + product
+    for copy in load_downs:
+        copy.wait()
+    lows = dot_t(normed[...], down_v[...])
+    lows_t = lows.T
+    k_ref[...] = rows_v[:, COLS : 2 * COLS].astype(BF16)
+    for i, (target, up) in enumerate(((q_ref, bq_ref), (v_ref, bv_ref))):
+        ranks = slice(i * RANK, (i + 1) * RANK)
+        high, rest = split_high_low(lows[:, ranks])
+        u3[i] = jnp.concatenate([high, high, rest], axis=1)
+        high, rest = split_high_low(lows_t[ranks])
+        ut[i] = jnp.concatenate([high, rest], axis=0)
+        high, rest = split_high_low(up[...])
+        stacked = jnp.concatenate([high, rest, high], axis=0)
+        rows = rows_v[:, 2 * i * COLS : (2 * i + 1) * COLS]
+        target[...] = (rows + ADAPTER_SCALE * dot(u3[i], stacked)).astype(BF16)
 
     limit = len_ref[0]
     row = lax.broadcasted_iota(jnp.int32, (ROWS, ROWS), 0)
@@ -180,27 +288,18 @@
         mixed = dot(probs.astype(BF16), v_ref[:, lanes]).astype(BF16)
         dmcat[:, lanes] = mixed
         e1s[h] = mixed.astype(F32)
-    for i, ref in enumerate((uq_ref, uv_ref)):
-        high, low = split_high_low(ref[...])
-        u3[i] = jnp.concatenate([high, high, low], axis=1)
-    for i, ref in enumerate((uqt_ref, uvt_ref)):
-        high, low = split_high_low(ref[...])
-        ut[i] = jnp.concatenate([high, low], axis=0)
     place = lax.broadcasted_iota(jnp.int32, (ROWS, LANES), 0)
     mask_z = (place < limit).astype(F32)
     mask_x = (place[:HALF] + x * HALF < limit).astype(F32)
+    for copy in load_targets:
+        copy.wait()
     for s in range(STAGES):
-        cprev_x[s] = gap_x_ref[s] * mask_x
-        cprev_z[s] = gap_z_ref[s] * mask_z
+        gap = inputs_v[half_rows, gap_lanes(s, 0)].astype(F32) - targets_x[s].astype(F32)
+        cprev_x[s] = gap * mask_x
+        gap = inputs_v[:, gap_lanes(s, 1)].astype(F32) - targets_z[s].astype(F32)
+        cprev_z[s] = gap * mask_z
     state[...] = jnp.zeros_like(state)
     sca[...] = jnp.zeros_like(sca)
-
-    @pl.loop(0, CHUNKS)
-    def _(j):
-        own_copy(j).wait()
-        w_copy(j).wait_recv()
-        wb[j, pl.ds(COLS, COLS)] = wrecv[j].astype(BF16)
-        w_copy(j).wait_send()
 
     @pl.loop(0, CG_STEPS + 1)
     def _(k):
@@ -252,9 +351,20 @@
         def x1(s):
             return remote(part_x.at[s, 1 - x], rx1.at[s], S_X1 + s, R_X1 + s, xn)
 
-        def z1(s, off):
-            i = 3 * s + off - 1
-            return remote(part_z.at[s, zi(off)], rz1.at[s, off - 1], S_Z1 + i, R_Z1 + i, zn(off))
+        upper, lower = pl.ds(0, HALF), pl.ds(HALF, HALF)
+
+        def z1(s, role):
+            to, row, target = (
+                (2, upper, rz0.at[s, 0]),
+                (2, lower, rz0.at[s, 1]),
+                (1, lower, rz1.at[s, 0, lower]),
+                (3, upper, rz1.at[s, 1, upper]),
+                (1, upper, rz1.at[s, 0, upper]),
+                (3, lower, rz1.at[s, 1, lower]),
+            )[role]
+            i = 6 * s + role
+            source = part_z.at[s, zi(to), row]
+            return remote(source, target, S_Z1 + i, R_Z1 + i, zn(1 if role % 2 == 0 else 3))
 
         def x2(s, off):
             i = 3 * s + off - 1
@@ -264,11 +374,20 @@
             return remote(part_z.at[s, z], rz2.at[s], S_Z2 + s, R_Z2 + s, xn)
 
         for s in range(STAGES):
+
+            @pl.when(k == 0)
+            def _():
+                for off in (2, 3, 0, 1):
+                    j = s * N_Z + zi(off)
+                    own_copy(j).wait()
+                    w_copy(j).wait_recv()
+                    wb[j, pl.ds(COLS, COLS)] = wrecv[j].astype(BF16)
+
             for off in (2, 1, 3, 0):
                 product = dot(dmcat[...], wb[s * N_Z + zi(off)])
                 part_z[s, zi(off)] = product[:, LANES:]
-                if off:
-                    z1(s, off).start()
+                for role in ((), (2,), (0, 1), (3,))[off]:
+                    z1(s, role).start()
                 part_x[s, 0, zi(off)] = product[:HALF, :LANES]
                 part_x[s, 1, zi(off)] = product[HALF:, :LANES]
             x1(s).start()
@@ -283,14 +402,31 @@
             s3(off, z).start()
 
         for s in range(STAGES):
+            z1(s, 0).wait_recv()
+            part_z[s, zi(1), :HALF] = part_z[s, zi(1), :HALF] + rz0[s, 0]
+            z1(s, 4).start()
+            z1(s, 1).wait_recv()
+            part_z[s, zi(3), HALF:] = part_z[s, zi(3), HALF:] + rz0[s, 1]
+            z1(s, 5).start()
+
+        def second_x(s):
             x1(s).wait_recv()
             part_x[s, x] = part_x[s, x] + rx1[s]
             for off in (2, 1, 3):
                 x2(s, off).start()
-            for off in (1, 2, 3):
-                z1(s, off).wait_recv()
-            part_z[s, z] = part_z[s, z] + rz1[s, 0] + rz1[s, 1] + rz1[s, 2]
+
+        def second_z(s):
+            for role in (2, 3, 4, 5):
+                z1(s, role).wait_recv()
+            part_z[s, z] = part_z[s, z] + rz1[s, 0] + rz1[s, 1]
             z2(s).start()
+
+        second_x(0)
+        second_z(0)
+        second_x(1)
+        second_z(1)
+        second_z(2)
+        second_x(2)
 
         for off in (1, 2, 3):
             s3(off, zi(off)).wait_recv()
@@ -305,12 +441,28 @@
             block = gx.at[s, x, peer]
             return remote(block, block, S_X3 + 3 * s + off - 1, R_X3 + N_Z * s + peer, zn(off))
 
-        def x4(s, half):
-            return remote(gx.at[s, half], gx.at[s, half], S_X4 + s, R_X4 + s, xn)
-
-        def z4(s, off, peer):
-            block = gz.at[s, peer]
-            return remote(block, block, S_Z4 + 3 * s + off - 1, R_Z4 + N_Z * s + peer, zn(off))
+        def x4(s, half, peer):
+            block = gx.at[s, half, peer]
+            i = N_Z * s + peer
+            return remote(block, block, S_X4 + i, R_X4 + i, xn)
+
+        def z4(s, role, incoming=False):
+            if incoming:
+                block = (
+                    gz.at[s, zi(3)],
+                    gz.at[s, zi(1)],
+                    gz.at[s, zi(2), upper],
+                    gz.at[s, zi(2), lower],
+                )[role]
+            else:
+                block = (
+                    gz.at[s, z],
+                    gz.at[s, z],
+                    gz.at[s, zi(3), upper],
+                    gz.at[s, zi(1), lower],
+                )[role]
+            i = 4 * s + role
+            return remote(block, block, S_Z4 + i, R_Z4 + i, zn(1 if role % 2 == 0 else 3))
 
         def own_x(s):
             for off in (1, 2, 3):
@@ -321,6 +473,7 @@
             gx[s, x, z] = block
             for off in (2, 1, 3):
                 x3(s, off, z).start()
+            x4(s, x, z).start()
 
         def own_z(s):
             z2(s).wait_recv()
@@ -328,27 +481,40 @@
             block = block * mask_z + beta_row * cprev_z[s]
             cprev_z[s] = block
             gz[s, z] = block
-            for off in (2, 1, 3):
-                z4(s, off, z).start()
+            z4(s, 0).start()
+            z4(s, 1).start()
+
+        def pass_x(s):
+            for off in (1, 3, 2):
+                x3(s, off, zi(off)).wait_recv()
+                x4(s, x, zi(off)).start()
+
+        def pass_z(s):
+            for role in range(2):
+                z4(s, role, True).wait_recv()
+                z4(s, role + 2).start()
 
         own_x(0)
+        own_z(0)
         own_x(1)
-        own_z(0)
-        own_x(2)
         own_z(1)
         own_z(2)
+        pass_x(0)
+        own_x(2)
         state[1] = state[0] + beta_row * state[1]
-        for s in range(STAGES):
-            for off in (1, 3, 2):
-                x3(s, off, zi(off)).wait_recv()
-            x4(s, x).start()
+        pass_z(0)
+        pass_x(1)
+        pass_z(1)
+        pass_z(2)
+        pass_x(2)
 
         squares[...] = jnp.zeros_like(squares)
         for s in range(STAGES):
-            x4(s, 1 - x).wait_recv()
             for off in (0, 1, 3, 2):
-                if off:
-                    z4(s, off, zi(off)).wait_recv()
+                x4(s, 1 - x, zi(off)).wait_recv()
+                if off == 2:
+                    z4(s, 2, True).wait_recv()
+                    z4(s, 3, True).wait_recv()
                 left = jnp.concatenate([gx[s, 0, zi(off)], gx[s, 1, zi(off)]], axis=0)
                 both = jnp.concatenate([left, gz[s, zi(off)]], axis=1)
                 product = dot_t(both.astype(BF16), wb[s * N_Z + zi(off)])
@@ -408,12 +574,14 @@
         for s in range(STAGES):
             x1(s).wait_send()
             z2(s).wait_send()
-            x4(s, x).wait_send()
             for off in (1, 2, 3):
-                z1(s, off).wait_send()
                 x2(s, off).wait_send()
                 x3(s, off, z).wait_send()
-                z4(s, off, z).wait_send()
+            for peer in range(N_Z):
+                x4(s, x, peer).wait_send()
+                z4(s, peer).wait_send()
+            for role in range(6):
+                z1(s, role).wait_send()
         e2.wait_send()
         s6.wait_send()
 
@@ -437,16 +605,28 @@
         state[0] = state[0] - alpha * image
         sca[1] = sca[0]
 
+    for j in range(CHUNKS):
+        w_copy(j).wait_send()
     step_ref[...] = state[2]
     remain_ref[...] = state[0]
 
 
-def solve(lengths, q, k, v, uq, uv, gap_x, gap_z, w_out):
+def solve(lengths, gain, bias, bq, bv, inputs, targets, wq, wk, wv, dq, dv, w_out):
     vmem = pl.BlockSpec(memory_space=pltpu.VMEM)
     square = (HEADS, HEAD_DIM, HEAD_DIM)
     half_block = (HALF, LANES)
     block = (ROWS, LANES)
     scratch = [
+        pltpu.VMEM((ROWS, WIDTH), BF16),
+        pltpu.VMEM((STAGES,) + half_block, BF16),
+        pltpu.VMEM((STAGES,) + block, BF16),
+        pltpu.VMEM((ROWS, WIDTH), BF16),
+        pltpu.VMEM((WIDTH, 3 * COLS), BF16),
+        pltpu.VMEM((ROWS, 3 * COLS), F32),
+        pltpu.VMEM((2 * RANK, WIDTH), BF16),
+        pltpu.VMEM((ROWS, COLS), BF16),
+        pltpu.VMEM((ROWS, COLS), BF16),
+        pltpu.VMEM((ROWS, COLS), BF16),
         pltpu.VMEM((CHUNKS, 2 * COLS, PAIR), BF16),
         pltpu.VMEM((CHUNKS, COLS, PAIR), BF16),
         pltpu.VMEM((CHUNKS, COLS, PAIR), F32),
@@ -462,7 +642,8 @@
         pltpu.VMEM((STAGES, 2, N_Z) + half_block, F32),
         pltpu.VMEM((STAGES, N_Z) + block, F32),
         pltpu.VMEM((STAGES, N_Z) + half_block, F32),
-        pltpu.VMEM((STAGES, N_Z - 1) + block, F32),
+        pltpu.VMEM((STAGES, 2) + half_block, F32),
+        pltpu.VMEM((STAGES, 2) + block, F32),
         pltpu.VMEM((STAGES, N_Z - 1) + half_block, F32),
         pltpu.VMEM((STAGES,) + block, F32),
         pltpu.VMEM((STAGES, 2, N_Z) + half_block, F32),
@@ -481,6 +662,7 @@
         pltpu.VMEM((N_Z, 2, 8, 128), F32),
         pltpu.VMEM((8, 128), F32),
         pltpu.SemaphoreType.DMA((2 * CHUNKS,)),
+        pltpu.SemaphoreType.DMA((36,)),
         pltpu.SemaphoreType.DMA((N_SEND,)),
         pltpu.SemaphoreType.DMA((N_RECV,)),
     ]
@@ -489,25 +671,18 @@
         kernel,
         out_shape=(shape, shape),
         in_specs=[pl.BlockSpec(memory_space=pltpu.SMEM)]
-        + [vmem] * 9
-        + [pl.BlockSpec(memory_space=pl.ANY)],
+        + [vmem] * 4
+        + [pl.BlockSpec(memory_space=pl.ANY)] * 8,
         out_specs=(vmem, vmem),
         scratch_shapes=scratch,
         compiler_params=pltpu.CompilerParams(
-            collective_id=0, has_side_effects=True, vmem_limit_bytes=48 * 2**20
+            collective_id=0, has_side_effects=True, vmem_limit_bytes=58 * 2**20
         ),
         cost_estimate=pl.CostEstimate(
             flops=8 * 2 * ROWS * WIDTH * COLS, bytes_accessed=8 * 2**20, transcendentals=0
         ),
         name="newton",
-    )(lengths, q, k, v, uq, uv, uq.T, uv.T, gap_x, gap_z, w_out)
-
-
-def layer_norm(rows, gain, bias):
-    rows = rows.astype(F32)
-    centred = rows - jnp.mean(rows, axis=-1, keepdims=True)
-    spread = jnp.mean(centred * centred, axis=-1, keepdims=True)
-    return (centred * lax.rsqrt(spread + EPS) * gain + bias).astype(BF16)
+    )(lengths, gain, bias, bq, bv, inputs, targets, wq, wk, wv, dq, dv, w_out)
 
 
 def on_device(
@@ -525,33 +700,21 @@
     query_up_factor,
     value_up_factor,
 ):
-    normed = layer_norm(inputs, ln_gain, ln_bias)
-    downs = jnp.concatenate([down_query, down_value], axis=1)
-    both = jnp.dot(normed, downs, preferred_element_type=F32)
-    uq, uv = both[:, :RANK], both[:, RANK:]
-
-    def project(weight, low, up):
-        rows = jnp.dot(normed, weight, preferred_element_type=F32)
-        if up is not None:
-            rows = rows + ADAPTER_SCALE * jnp.dot(low, up, precision=lax.Precision.HIGHEST)
-        return rows.astype(BF16)
-
-    q = project(query_weight, uq, query_up_factor)
-    k = project(w_key, None, None)
-    v = project(value_weight, uv, value_up_factor)
-
-    t = lax.axis_index("tensor")
-    gaps_x, gaps_z = [], []
-    for s in range(STAGES):
-        left = t % 2 * CORE_WIDTH + (s * N_Z + t // 4) * PAIR
-        top = (t // 2) % 2 * HALF
-        for gaps, size, at in (
-            (gaps_x, (HALF, LANES), (top, left)),
-            (gaps_z, (ROWS, LANES), (0, left + LANES)),
-        ):
-            parts = [lax.dynamic_slice(a, at, size) for a in (inputs, targets)]
-            gaps.append(parts[0].astype(F32) - parts[1].astype(F32))
-    step, remain = solve(lengths, q, k, v, uq, uv, jnp.stack(gaps_x), jnp.stack(gaps_z), w_out)
+    step, remain = solve(
+        lengths,
+        ln_gain.reshape(1, WIDTH),
+        ln_bias.reshape(1, WIDTH),
+        query_up_factor,
+        value_up_factor,
+        inputs,
+        targets,
+        query_weight,
+        w_key,
+        value_weight,
+        down_query.T,
+        down_value.T,
+        w_out,
+    )
     return (step[:RANK], step[RANK:], remain[:RANK], remain[RANK:])
 
 

time: 197 us -> 178 us (0.904)
  other arithmetic: 6.16 us -> 0 us
  Pallas kernels: 181 us -> 175 us
  matrix products: 4.34 us -> 0 us
  local copies, waits for them, and re-layouts: 3.45 us -> 1.43 us
    pallas_call x1, Pallas kernels: 181 us -> 175 us  [solve(): pl.pallas_call(kernel, out_shape=(shape, shape), in_specs=[pl.BlockSpec(m...]
    dot_general x6 -> x0, matrix products: 4.34 us -> none  [the longest x3 2.97 us: project(): rows = jnp.dot(normed, weight, preferred_element_type=F32)]
    reduce_sum x2 -> x0, other arithmetic: 3.83 us -> none  [the longest x1 1.98 us: layer_norm(): spread = jnp.mean(centred * centred, axis=-1, keepdims=True)]
    unnamed x26 -> x0, local copies, waits for them, and re-layouts: 2.61 us -> none
where the time goes in v3:
time: 178 us
  Pallas kernels  175 us (98%)
    pallas_call x1, Pallas kernels, solve(): pl.pallas_call(kernel, out_shape=(shape, shape), in_specs=[pl.BlockSpec(m...  175 us

profile of v3, /device:TPU:1, one launch (start us, length us, event | category | flops | bytes accessed | tf_op | source)
XLA Modules:
  0.0 177.5 jit_solution(10905136587788331428)
XLA Ops:
  1.3 174.8 %newton.1 = (f32[32,384]{1,0:T(8,128)}, f32[32,384]{1,0:T(8,128)}) custom-call(s32[1]{0:T(128)S(6)} %copy.17.len_ref, f32[1,6144]{1,0:T(1,128)} %bitcast.6, f32[1,6144]{1,0:T(1,128)} %bitcast.7, f32[16,384]{1,0:T(8,128)} %bq_ref.1, f32[16,384]{1,0:T(8,128)} %bv_ref.1, bf16[128,6144]{1,0:T(8,128)(2,1)} %inputs_ref.1, bf16[128,6144]{1,0:T(8,128)(2,1)} %targets_ref.1, ...), custom_call_target="tpu_custom_call" | custom-call | flops 4831838208 | bytes 8388608 | tf_op jit(solution)/shard_map/newton/pallas_call | solution.py:670
  176.1 1.4 fusion

commit v4 on v3

--- a/solution.py
+++ b/solution.py
@@ -32,9 +32,9 @@
 MESH = pl.DeviceIdType.MESH
 
 S_W, S_E1, S_S1, S_S2, S_S3, S_S6, S_E2, S_X1, S_Z1, S_X2 = 0, 12, 15, 16, 17, 20, 21, 22, 25, 43
-S_Z2, S_X3, S_X4, S_Z4, S_AR, S_SQ, N_SEND = 52, 55, 64, 76, 88, 95, 102
+S_Z2, S_X3, S_X4, S_Z4, S_AR, S_SQ, N_SEND = 52, 55, 64, 76, 88, 102, 109
 R_W, R_E1, R_S1, R_S2, R_S3, R_S6, R_E2, R_X1, R_Z1, R_X2 = 0, 12, 15, 16, 17, 21, 22, 23, 26, 44
-R_Z2, R_X3, R_X4, R_Z4, R_AR, R_SQ, N_RECV = 53, 56, 68, 80, 92, 108, 124
+R_Z2, R_X3, R_X4, R_Z4, R_AR, R_SQ, N_RECV = 53, 56, 68, 80, 92, 124, 140
 
 PEERS = ((1, 2), (1, 1), (1, 3), (0, 2), (1, 0), (0, 1), (0, 3))
 
@@ -92,6 +92,7 @@
     u3,
     ut,
     dmcat,
+    begun,
     e1s,
     e1r,
     part_x,
@@ -243,19 +244,17 @@
 
     pl.semaphore_wait(barrier, len(partners))
 
-    @pl.loop(0, CHUNKS)
-    def _(i):
-        j = order(i)
-        other_copy(j).wait()
-        wsend[j] = wtmp[j].astype(F32)
-        w_copy(j).start()
-
     for i, piece in enumerate(pieces):
-        for copy in piece:
+        given = [order(j) for j in range(3 * i // 2, 3 * (i + 1) // 2)]
+        for copy in piece + [other_copy(j) for j in given]:
             copy.wait()
         depth = pl.ds(i * DEPTH, DEPTH)
         product = dot(normed[:, depth], weights_v[depth, :])
+        for j in given:
+            wsend[j] = wtmp[j].astype(F32)
         rows_v[...] = product if i == 0 else rows_v[...] + product
+        for j in given:
+            w_copy(j).start()
     for copy in load_downs:
         copy.wait()
     lows = dot_t(normed[...], down_v[...])
@@ -276,18 +275,18 @@
     row = lax.broadcasted_iota(jnp.int32, (ROWS, ROWS), 0)
     col = lax.broadcasted_iota(jnp.int32, (ROWS, ROWS), 1)
     live = (col <= row) & (col < limit)
-    for h in range(HEADS):
-        lanes = pl.ds(h * HEAD_DIM, HEAD_DIM)
-        scores = dot_t(q_ref[:, lanes], k_ref[:, lanes]) * HEAD_DIM ** (-0.5)
-        scores = jnp.where(live, scores, NEG)
-        weights = jnp.exp(scores - jnp.max(scores, axis=-1, keepdims=True))
-        probs = weights / jnp.sum(weights, axis=-1, keepdims=True)
-        pf[h] = probs
-        pb[h] = probs.astype(BF16)
-        pbt[h] = probs.T.astype(BF16)
-        mixed = dot(probs.astype(BF16), v_ref[:, lanes]).astype(BF16)
-        dmcat[:, lanes] = mixed
-        e1s[h] = mixed.astype(F32)
+    lanes = [pl.ds(h * HEAD_DIM, HEAD_DIM) for h in range(HEADS)]
+    scores = [dot_t(q_ref[:, n], k_ref[:, n]) * HEAD_DIM ** (-0.5) for n in lanes]
+    scores = [jnp.where(live, a, NEG) for a in scores]
+    weights = [jnp.exp(a - jnp.max(a, axis=-1, keepdims=True)) for a in scores]
+    probs = [a / jnp.sum(a, axis=-1, keepdims=True) for a in weights]
+    mixed = [dot(a.astype(BF16), v_ref[:, n]).astype(BF16) for a, n in zip(probs, lanes)]
+    for h, n in enumerate(lanes):
+        pf[h] = probs[h]
+        pb[h] = probs[h].astype(BF16)
+        pbt[h] = probs[h].T.astype(BF16)
+        dmcat[:, n] = mixed[h]
+        e1s[:, n] = mixed[h].astype(F32)
     place = lax.broadcasted_iota(jnp.int32, (ROWS, LANES), 0)
     mask_z = (place < limit).astype(F32)
     mask_x = (place[:HALF] + x * HALF < limit).astype(F32)
@@ -303,43 +302,43 @@
 
     @pl.loop(0, CG_STEPS + 1)
     def _(k):
-        def e1(h):
-            return remote(e1s.at[h], e1r.at[h], S_E1 + h, R_E1 + h, sib)
-
         @pl.when(k > 0)
         def _():
-            remain = state[0]
             tangents = []
             for i in range(2):
-                high, low = split_high_low(remain[i * RANK : (i + 1) * RANK])
+                high, low = split_high_low(state[0, i * RANK : (i + 1) * RANK])
                 stacked = jnp.concatenate([high, low, high], axis=0)
                 tangents.append((ADAPTER_SCALE * dot(u3[i], stacked)).astype(BF16))
-            dq, dv = tangents
-            for h in range(HEADS):
-                lanes = slice(h * HEAD_DIM, (h + 1) * HEAD_DIM)
-                scores = dot_t(dq[:, lanes], k_ref[:, lanes]) * HEAD_DIM ** (-0.5)
-                probs = pf[h]
-                tilted = probs * scores
-                dprobs = tilted - probs * jnp.sum(tilted, axis=-1, keepdims=True)
-                left = jnp.concatenate([dprobs.astype(BF16), pb[h]], axis=1)
-                right = jnp.concatenate([v_ref[:, lanes], dv[:, lanes]], axis=0)
-                dmixed = dot(left, right).astype(BF16)
-                dmcat[:, lanes] = dmixed
-                e1s[h] = dmixed.astype(F32)
-                e1(h).start()
-
-        @pl.when(k == 0)
-        def _():
-            for h in range(HEADS):
-                e1(h).start()
-
+            dq, dv = [[a[:, h * HEAD_DIM : (h + 1) * HEAD_DIM] for h in range(HEADS)] for a in tangents]
+            scores = [dot_t(a, k_ref[:, n]) * HEAD_DIM ** (-0.5) for a, n in zip(dq, lanes)]
+            tilted = [pf[h] * a for h, a in enumerate(scores)]
+            dprobs = [
+                (a - pf[h] * jnp.sum(a, axis=-1, keepdims=True)).astype(BF16)
+                for h, a in enumerate(tilted)
+            ]
+            left = [jnp.concatenate([a, pb[h]], axis=1) for h, a in enumerate(dprobs)]
+            right = [jnp.concatenate([v_ref[:, n], a], axis=0) for a, n in zip(dv, lanes)]
+            dmixed = [dot(a, b).astype(BF16) for a, b in zip(left, right)]
+            for a, n in zip(dmixed, lanes):
+                e1s[:, n] = a.astype(F32)
+                dmcat[:, n] = a
+
+        e1 = remote(e1s, e1r, S_E1, R_E1, sib)
+        e1.start()
         sca[4] = jnp.broadcast_to(total(state[0] * state[0]), (8, 128))
         sca[5] = jnp.broadcast_to(total(state[0] * state[1]), (8, 128))
         s1 = remote(sca.at[pl.ds(4, 2)], s1r, S_S1, R_S1, sib)
         s1.start()
-        for h in range(HEADS):
-            e1(h).wait_recv()
-            dmcat[:, pl.ds(COLS + h * HEAD_DIM, HEAD_DIM)] = e1r[h].astype(BF16)
+        @pl.when(k == 0)
+        def _():
+            for j in range(CHUNKS):
+                own_copy(j).wait()
+
+        for s in range(STAGES):
+            for off in (2, 1, 3, 0):
+                begun[s, off] = dot(dmcat[:, :PAIR], wb[s * N_Z + lax.rem(z + off, N_Z), :PAIR])
+        e1.wait_recv()
+        dmcat[:, pl.ds(COLS, COLS)] = e1r[...].astype(BF16)
         s1.wait_recv()
         sca[pl.ds(6, 2)] = sca[pl.ds(4, 2)] + s1r[...]
         s2 = remote(sca.at[pl.ds(6, 2)], s2r, S_S2, R_S2, xn)
@@ -357,12 +356,10 @@
             to, row, target = (
                 (2, upper, rz0.at[s, 0]),
                 (2, lower, rz0.at[s, 1]),
-                (1, lower, rz1.at[s, 0, lower]),
-                (3, upper, rz1.at[s, 1, upper]),
-                (1, upper, rz1.at[s, 0, upper]),
-                (3, lower, rz1.at[s, 1, lower]),
+                (1, pl.ds(0, ROWS), rz1.at[s, 0]),
+                (3, pl.ds(0, ROWS), rz1.at[s, 1]),
             )[role]
-            i = 6 * s + role
+            i = 4 * s + role
             source = part_z.at[s, zi(to), row]
             return remote(source, target, S_Z1 + i, R_Z1 + i, zn(1 if role % 2 == 0 else 3))
 
@@ -379,14 +376,13 @@
             def _():
                 for off in (2, 3, 0, 1):
                     j = s * N_Z + zi(off)
-                    own_copy(j).wait()
                     w_copy(j).wait_recv()
                     wb[j, pl.ds(COLS, COLS)] = wrecv[j].astype(BF16)
 
             for off in (2, 1, 3, 0):
-                product = dot(dmcat[...], wb[s * N_Z + zi(off)])
+                product = begun[s, off] + dot(dmcat[:, PAIR:], wb[s * N_Z + zi(off), PAIR:])
                 part_z[s, zi(off)] = product[:, LANES:]
-                for role in ((), (2,), (0, 1), (3,))[off]:
+                for role in (0, 1) if off == 2 else ():
                     z1(s, role).start()
                 part_x[s, 0, zi(off)] = product[:HALF, :LANES]
                 part_x[s, 1, zi(off)] = product[HALF:, :LANES]
@@ -404,10 +400,10 @@
         for s in range(STAGES):
             z1(s, 0).wait_recv()
             part_z[s, zi(1), :HALF] = part_z[s, zi(1), :HALF] + rz0[s, 0]
-            z1(s, 4).start()
+            z1(s, 2).start()
             z1(s, 1).wait_recv()
             part_z[s, zi(3), HALF:] = part_z[s, zi(3), HALF:] + rz0[s, 1]
-            z1(s, 5).start()
+            z1(s, 3).start()
 
         def second_x(s):
             x1(s).wait_recv()
@@ -416,7 +412,7 @@
                 x2(s, off).start()
 
         def second_z(s):
-            for role in (2, 3, 4, 5):
+            for role in (2, 3):
                 z1(s, role).wait_recv()
             part_z[s, z] = part_z[s, z] + rz1[s, 0] + rz1[s, 1]
             z2(s).start()
@@ -495,18 +491,18 @@
                 z4(s, role + 2).start()
 
         own_x(0)
+        own_x(1)
         own_z(0)
-        own_x(1)
+        own_x(2)
         own_z(1)
         own_z(2)
         pass_x(0)
-        own_x(2)
-        state[1] = state[0] + beta_row * state[1]
+        pass_x(1)
         pass_z(0)
-        pass_x(1)
+        pass_x(2)
         pass_z(1)
         pass_z(2)
-        pass_x(2)
+        state[1] = state[0] + beta_row * state[1]
 
         squares[...] = jnp.zeros_like(squares)
         for s in range(STAGES):
@@ -533,10 +529,10 @@
 
         parity = lax.rem(k, 2)
 
-        def ar(i, peer):
-            block = arb.at[parity, peer]
-            r = R_AR + parity * N_DP + peer
-            return remote(block, block, S_AR + i, r, (dpn(PEERS[i]), t))
+        def ar(i, side, peer):
+            block = arb.at[parity, peer, side]
+            r = R_AR + (parity * N_DP + peer) * 2 + side
+            return remote(block, block, S_AR + 2 * i + side, r, (dpn(PEERS[i]), t))
 
         def sq(i, peer):
             block = sqb.at[parity, peer]
@@ -547,26 +543,24 @@
         for i in range(N_DP - 1):
             sq(i, d).start()
         e2.wait_recv()
-        for h in range(HEADS):
-            lanes = slice(h * HEAD_DIM, (h + 1) * HEAD_DIM)
-            cotan = (cot[:, lanes] + e2r[:, lanes]).astype(BF16)
-            dprobs = dot_t(cotan, v_ref[:, lanes])
-            probs = pf[h]
-            tilted = probs * dprobs
-            dscores = tilted - probs * jnp.sum(tilted, axis=-1, keepdims=True)
-            dscores = (dscores * HEAD_DIM ** (-0.5)).astype(BF16)
-            dq = dot(dscores, k_ref[:, lanes]).astype(BF16)
-            dv = dot(pbt[h], cotan).astype(BF16)
-            for i, cotangent in enumerate((dq, dv)):
-                both = dot(ut[i], cotangent)
-                arb[parity, d, i * RANK : (i + 1) * RANK, lanes] = ADAPTER_SCALE * (
-                    both[:RANK] + both[RANK:]
-                )
-        for i in range(N_DP - 1):
-            ar(i, d).start()
-
-        for h in range(HEADS):
-            e1(h).wait_send()
+        def gradient(side, cotangents):
+            both = dot(ut[side], jnp.concatenate(cotangents, axis=1))
+            arb[parity, d, side] = ADAPTER_SCALE * (both[:RANK] + both[RANK:])
+            for i in range(N_DP - 1):
+                ar(i, side, d).start()
+
+        cotan = (cot[:, :COLS] + e2r[...]).astype(BF16)
+        cotan = [cotan[:, h * HEAD_DIM : (h + 1) * HEAD_DIM] for h in range(HEADS)]
+        gradient(1, [dot(pbt[h], a).astype(BF16) for h, a in enumerate(cotan)])
+        dprobs = [dot_t(a, v_ref[:, n]) for a, n in zip(cotan, lanes)]
+        tilted = [pf[h] * a for h, a in enumerate(dprobs)]
+        dscores = [
+            ((a - pf[h] * jnp.sum(a, axis=-1, keepdims=True)) * HEAD_DIM ** (-0.5)).astype(BF16)
+            for h, a in enumerate(tilted)
+        ]
+        gradient(0, [dot(a, k_ref[:, n]).astype(BF16) for a, n in zip(dscores, lanes)])
+
+        e1.wait_send()
         s1.wait_send()
         s2.wait_send()
         for off in (1, 2, 3):
@@ -580,20 +574,23 @@
             for peer in range(N_Z):
                 x4(s, x, peer).wait_send()
                 z4(s, peer).wait_send()
-            for role in range(6):
+            for role in range(4):
                 z1(s, role).wait_send()
         e2.wait_send()
         s6.wait_send()
 
         for i in reversed(range(N_DP - 1)):
-            ar(i, dpn(PEERS[i])).wait_recv()
             sq(i, dpn(PEERS[i])).wait_recv()
+            for side in range(2):
+                ar(i, side, dpn(PEERS[i])).wait_recv()
         for i in range(N_DP - 1):
-            ar(i, d).wait_send()
             sq(i, d).wait_send()
-        summed = arb[parity, 0]
+            for side in range(2):
+                ar(i, side, d).wait_send()
+        summed = [arb[parity, 0, side] for side in range(2)]
         for peer in range(1, N_DP):
-            summed = summed + arb[parity, peer]
+            summed = [a + arb[parity, peer, side] for side, a in enumerate(summed)]
+        summed = jnp.concatenate(summed, axis=0)
         image = summed * (1.0 / (ROWS * N_DP)) + DAMP * state[1]
         squared = sqb[parity, 0]
         for peer in range(1, N_DP):
@@ -637,8 +634,9 @@
         pltpu.VMEM((2, ROWS, 3 * RANK), BF16),
         pltpu.VMEM((2, 2 * RANK, ROWS), BF16),
         pltpu.VMEM((ROWS, 2 * COLS), BF16),
-        pltpu.VMEM(square, F32),
-        pltpu.VMEM(square, F32),
+        pltpu.VMEM((STAGES, N_Z, ROWS, PAIR), F32),
+        pltpu.VMEM((ROWS, COLS), F32),
+        pltpu.VMEM((ROWS, COLS), F32),
         pltpu.VMEM((STAGES, 2, N_Z) + half_block, F32),
         pltpu.VMEM((STAGES, N_Z) + block, F32),
         pltpu.VMEM((STAGES, N_Z) + half_block, F32),
@@ -652,7 +650,7 @@
         pltpu.VMEM((STAGES,) + block, F32),
         pltpu.VMEM((ROWS, 2 * COLS), F32),
         pltpu.VMEM((ROWS, COLS), F32),
-        pltpu.VMEM((2, N_DP, 2 * RANK, COLS), F32),
+        pltpu.VMEM((2, N_DP, 2, RANK, COLS), F32),
         pltpu.VMEM((2, N_DP, 8, 128), F32),
         pltpu.VMEM((ROWS, PAIR), F32),
         pltpu.VMEM((3, 2 * RANK, COLS), F32),

time: 178 us -> 173 us (0.972)
  Pallas kernels: 175 us -> 170 us
    pallas_call x1, Pallas kernels: 175 us -> 170 us  [solve(): pl.pallas_call(kernel, out_shape=(shape, shape), in_specs=[pl.BlockSpec(m...]
where the time goes in v4:
time: 173 us
  Pallas kernels  170 us (98%)
    pallas_call x1, Pallas kernels, solve(): pl.pallas_call(kernel, out_shape=(shape, shape), in_specs=[pl.BlockSpec(m...  170 us

profile of v4, /device:TPU:1, one launch (start us, length us, event | category | flops | bytes accessed | tf_op | source)
XLA Modules:
  0.0 173.1 jit_solution(4250154716163885726)
XLA Ops:
  1.3 170.3 %newton.1 = (f32[32,384]{1,0:T(8,128)}, f32[32,384]{1,0:T(8,128)}) custom-call(s32[1]{0:T(128)S(6)} %copy.17.len_ref, f32[1,6144]{1,0:T(1,128)} %bitcast.6, f32[1,6144]{1,0:T(1,128)} %bitcast.7, f32[16,384]{1,0:T(8,128)} %bq_ref.1, f32[16,384]{1,0:T(8,128)} %bv_ref.1, bf16[128,6144]{1,0:T(8,128)(2,1)} %inputs_ref.1, bf16[128,6144]{1,0:T(8,128)(2,1)} %targets_ref.1, ...), custom_call_target="tpu_custom_call" | custom-call | flops 4831838208 | bytes 8388608 | tf_op jit(solution)/shard_map/newton/pallas_call | solution.py:668
  171.6 1.4 fusion

commit v5 on v4

--- a/solution.py
+++ b/solution.py
@@ -31,10 +31,10 @@
 BF16 = jnp.bfloat16
 MESH = pl.DeviceIdType.MESH
 
-S_W, S_E1, S_S1, S_S2, S_S3, S_S6, S_E2, S_X1, S_Z1, S_X2 = 0, 12, 15, 16, 17, 20, 21, 22, 25, 43
-S_Z2, S_X3, S_X4, S_Z4, S_AR, S_SQ, N_SEND = 52, 55, 64, 76, 88, 102, 109
-R_W, R_E1, R_S1, R_S2, R_S3, R_S6, R_E2, R_X1, R_Z1, R_X2 = 0, 12, 15, 16, 17, 21, 22, 23, 26, 44
-R_Z2, R_X3, R_X4, R_Z4, R_AR, R_SQ, N_RECV = 53, 56, 68, 80, 92, 124, 140
+S_W, S_E1, S_S1, S_S2, S_S3, S_S6, S_E2, S_X1, S_Z1, S_X2 = 0, 12, 15, 16, 17, 20, 21, 22, 34, 46
+S_Z2, S_X3, S_X4, S_Z4, S_AR, S_SQ, N_SEND = 55, 58, 67, 79, 91, 105, 112
+R_W, R_E1, R_S1, R_S2, R_S3, R_S6, R_E2, R_X1, R_Z1, R_X2 = 0, 12, 15, 16, 17, 21, 22, 23, 35, 47
+R_Z2, R_X3, R_X4, R_Z4, R_AR, R_SQ, N_RECV = 56, 59, 71, 83, 95, 127, 143
 
 PEERS = ((1, 2), (1, 1), (1, 3), (0, 2), (1, 0), (0, 1), (0, 3))
 
@@ -231,6 +231,17 @@
             for late in load_targets:
                 late.start()
 
+        if i == 1:
+            pl.semaphore_wait(barrier, len(partners))
+        if i:
+
+            @pl.loop(4 * (i - 1), 4 * i)
+            def _(n):
+                j = order(n)
+                other_copy(j).wait()
+                wsend[j] = wtmp[j].astype(F32)
+                w_copy(j).start()
+
         size = ROWS // len(load_inputs)
 
         @pl.loop(i * size // 16, (i + 1) * size // 16)
@@ -242,19 +253,12 @@
             scaled = centred * lax.rsqrt(spread + EPS)
             normed[rows, :] = (scaled * gain_ref[...] + bias_ref[...]).astype(BF16)
 
-    pl.semaphore_wait(barrier, len(partners))
-
     for i, piece in enumerate(pieces):
-        given = [order(j) for j in range(3 * i // 2, 3 * (i + 1) // 2)]
-        for copy in piece + [other_copy(j) for j in given]:
+        for copy in piece:
             copy.wait()
         depth = pl.ds(i * DEPTH, DEPTH)
         product = dot(normed[:, depth], weights_v[depth, :])
-        for j in given:
-            wsend[j] = wtmp[j].astype(F32)
         rows_v[...] = product if i == 0 else rows_v[...] + product
-        for j in given:
-            w_copy(j).start()
     for copy in load_downs:
         copy.wait()
     lows = dot_t(normed[...], down_v[...])
@@ -347,8 +351,10 @@
         def zi(off):
             return lax.rem(z + off, N_Z)
 
-        def x1(s):
-            return remote(part_x.at[s, 1 - x], rx1.at[s], S_X1 + s, R_X1 + s, xn)
+        def x1(s, off):
+            i = N_Z * s + off
+            source, target = part_x.at[s, 1 - x, zi(off)], rx1.at[s, zi(off)]
+            return remote(source, target, S_X1 + i, R_X1 + i, xn)
 
         upper, lower = pl.ds(0, HALF), pl.ds(HALF, HALF)
 
@@ -386,7 +392,7 @@
                     z1(s, role).start()
                 part_x[s, 0, zi(off)] = product[:HALF, :LANES]
                 part_x[s, 1, zi(off)] = product[HALF:, :LANES]
-            x1(s).start()
+                x1(s, off).start()
 
         s2.wait_recv()
         s3b[z] = sca[pl.ds(6, 2)] + s2r[...]
@@ -406,10 +412,11 @@
             z1(s, 3).start()
 
         def second_x(s):
-            x1(s).wait_recv()
-            part_x[s, x] = part_x[s, x] + rx1[s]
-            for off in (2, 1, 3):
-                x2(s, off).start()
+            for off in (2, 1, 3, 0):
+                x1(s, off).wait_recv()
+                part_x[s, x, zi(off)] = part_x[s, x, zi(off)] + rx1[s, zi(off)]
+                if off:
+                    x2(s, off).start()
 
         def second_z(s):
             for role in (2, 3):
@@ -566,7 +573,8 @@
         for off in (1, 2, 3):
             s3(off, z).wait_send()
         for s in range(STAGES):
-            x1(s).wait_send()
+            for off in range(N_Z):
+                x1(s, off).wait_send()
             z2(s).wait_send()
             for off in (1, 2, 3):
                 x2(s, off).wait_send()

time: 173 us -> 173 us (level)
  no operation moved by 1% of the time
where the time goes in v5:
time: 173 us; the launch traced here: 172 us
  Pallas kernels  170 us (98%)
    pallas_call x1, Pallas kernels, solve(): pl.pallas_call(kernel, out_shape=(shape, shape), in_specs=[pl.BlockSpec(m...  170 us

profile of v5, /device:TPU:1, one launch (start us, length us, event | category | flops | bytes accessed | tf_op | source)
XLA Modules:
  0.0 172.4 jit_solution(199440394010733587)
XLA Ops:
  1.3 169.7 %newton.1 = (f32[32,384]{1,0:T(8,128)}, f32[32,384]{1,0:T(8,128)}) custom-call(s32[1]{0:T(128)S(6)} %copy.17.len_ref, f32[1,6144]{1,0:T(1,128)} %bitcast.6, f32[1,6144]{1,0:T(1,128)} %bitcast.7, f32[16,384]{1,0:T(8,128)} %bq_ref.1, f32[16,384]{1,0:T(8,128)} %bv_ref.1, bf16[128,6144]{1,0:T(8,128)(2,1)} %inputs_ref.1, bf16[128,6144]{1,0:T(8,128)(2,1)} %targets_ref.1, ...), custom_call_target="tpu_custom_call" | custom-call | flops 4831838208 | bytes 8388608 | tf_op jit(solution)/shard_map/newton/pallas_call | solution.py:676
  171.0 1.4 fusion

commit v6 on v5

--- a/solution.py
+++ b/solution.py
@@ -428,8 +428,8 @@
         second_z(0)
         second_x(1)
         second_z(1)
+        second_x(2)
         second_z(2)
-        second_x(2)
 
         for off in (1, 2, 3):
             s3(off, zi(off)).wait_recv()

time: 173 us -> 173 us (level)
  no operation moved by 1% of the time
where the time goes in v6:
time: 173 us
  Pallas kernels  170 us (98%)
    pallas_call x1, Pallas kernels, solve(): pl.pallas_call(kernel, out_shape=(shape, shape), in_specs=[pl.BlockSpec(m...  170 us

profile of v6, /device:TPU:1, one launch (start us, length us, event | category | flops | bytes accessed | tf_op | source)
XLA Modules:
  0.0 172.6 jit_solution(8720685169593318693)
XLA Ops:
  1.3 169.9 %newton.1 = (f32[32,384]{1,0:T(8,128)}, f32[32,384]{1,0:T(8,128)}) custom-call(s32[1]{0:T(128)S(6)} %copy.17.len_ref, f32[1,6144]{1,0:T(1,128)} %bitcast.6, f32[1,6144]{1,0:T(1,128)} %bitcast.7, f32[16,384]{1,0:T(8,128)} %bq_ref.1, f32[16,384]{1,0:T(8,128)} %bv_ref.1, bf16[128,6144]{1,0:T(8,128)(2,1)} %inputs_ref.1, bf16[128,6144]{1,0:T(8,128)(2,1)} %targets_ref.1, ...), custom_call_target="tpu_custom_call" | custom-call | flops 4831838208 | bytes 8388608 | tf_op jit(solution)/shard_map/newton/pallas_call | solution.py:676
  171.2 1.4 fusion
